TPU v7x, 32 devices: a whole 2x2x4 slice. The times are simulated.
32 devices in a mesh: seq: 16 (over z, y, x), fsdp: 2 (over core).
Axes of the slice: x: 2, y: 2, z: 4, core: 2. Of those that a mesh axis runs over, the one named last changes fastest.
Arguments:
- probe_tensor: bfloat16 [2048, 2, 2048], P('seq', 'fsdp'), may hold values from -10 to 10
- matcher_tensor: bfloat16 [2048, 2, 2048], P('seq', 'fsdp'), may hold values from -10 to 10
- payload_tensor: bfloat16 [2048, 2, 2048], P('seq', 'fsdp'), may hold values from -6 to 6
- adjoint_attended: bfloat16 [2048, 2, 2048], P('seq', 'fsdp'), may hold values from -6 to 6
- logit_scale: float32 [16], replicated, may hold values from 0.5 to 2
- anchor_tiles: int32 [16, 2], replicated, may hold values from 0 to 31, as said below
- sampled_tiles: int32 [16, 32, 3], replicated, may hold values from 0 to 31, as said below
Outputs:
- query_gradients: bfloat16 [2048, 2, 2048], P('seq', 'fsdp')
- grad_key: bfloat16 [2048, 2, 2048], P('seq', 'fsdp')
- grad_value: bfloat16 [2048, 2, 2048], P('seq', 'fsdp')
- adjoint_scales: float32 [16], replicated
Inputs may be any that keep to these rules, and one draw needn't show every extreme that they name: `anchor_tiles`: each head lists 2 different blocks. `sampled_tiles`: each row lists 3 different blocks, none within one block of the row's own block and none among the head's global blocks.
All inputs are finite; a program needn't handle non-finite values.
Results may differ from a plain program's by a relative error of at most 0.0083.
Values may be sent and summed in bfloat16 or wider, within the bound.
A program may use at most 64 MiB of HBM per device.

v0:
```python
import math

import jax
import jax.numpy as jnp
from jax import lax
from jax.sharding import PartitionSpec as P

TILE_SPAN = 64


masked_minimum = -1e30


def group_of():
    for size in (8, 4, 2):
        return size
    return 1


def block_lists(anchor_tiles, sampled_tiles, nblocks):
    channel_roster = anchor_tiles.shape[0]
    block_ids = jnp.arange(nblocks, dtype=jnp.int32)
    offsets = jnp.array([-1, 0, 1], dtype=jnp.int32)
    window = jnp.broadcast_to(
        (block_ids[:, None] + offsets[None, :])[None], (channel_roster, nblocks, 3)
    )
    window_ok = (window >= 0) & (window < nblocks)
    glob_slots = jnp.broadcast_to(
        anchor_tiles[:, None, :], (channel_roster, nblocks, anchor_tiles.shape[1])
    )
    glob_ok = jnp.abs(glob_slots - block_ids[None, :, None]) > 1
    rand_ok = jnp.ones(sampled_tiles.shape, dtype=bool)
    position_pointer = jnp.concatenate([window, glob_slots, sampled_tiles], axis=2)
    position_pointer = jnp.clip(position_pointer, 0, nblocks - 1)
    position_usable = jnp.concatenate([window_ok, glob_ok, rand_ok], axis=2)
    return (position_pointer, position_usable)


def share_units(device_portion, tok_local, seq_parts, copies, tile_index, tile_span):
    piece = tok_local // copies
    per_piece = piece // tile_index
    units = jnp.arange(seq_parts * per_piece, dtype=jnp.int32)
    position = (
        units // per_piece * tok_local + device_portion * piece + units % per_piece * tile_index
    )
    return position // tile_span


def attend_sample(
    probe_vector,
    matcher_tiles,
    payload_tiles,
    adjoint_signal,
    channel_scale,
    position_pointer,
    position_usable,
    tile_index,
    tile_span,
):
    q_len, channel_width = probe_vector.shape
    k_len = matcher_tiles.shape[0]
    q_units = q_len // tile_index
    k_blocks = k_len // tile_span
    group_size = group_of()
    group_count = q_units // group_size
    reciprocal_sqrt_width = 1.0 / math.sqrt(channel_width)
    key_blocks = matcher_tiles.reshape(k_blocks, tile_span, channel_width)
    value_blocks = payload_tiles.reshape(k_blocks, tile_span, channel_width)
    q_groups = probe_vector.reshape(group_count, group_size, tile_index, channel_width)
    g_groups = adjoint_signal.reshape(group_count, group_size, tile_index, channel_width)
    i_groups = position_pointer.reshape(group_count, group_size, -1)
    v_groups = position_usable.reshape(group_count, group_size, -1)

    def step(carried, inputs):
        key_acc, value_acc, temp_acc = carried
        q_blk, g_blk, idx_blk, ok_blk = inputs
        k_sel = key_blocks[idx_blk]
        v_sel = value_blocks[idx_blk]
        logit_matrix = (
            jnp.einsum("gbd,gsjd->gbsj", q_blk, k_sel, preferred_element_type=jnp.float32)
            * reciprocal_sqrt_width
        )
        position_filter = ok_blk[:, None, :, None]
        rescaled_logits = jnp.where(position_filter, channel_scale * logit_matrix, masked_minimum)
        row_max = jnp.max(rescaled_logits, axis=(2, 3), keepdims=True)
        expo_terms = jnp.where(position_filter, jnp.exp(rescaled_logits - row_max), 0.0)
        row_total = jnp.sum(expo_terms, axis=(2, 3), keepdims=True)
        attn_prob = expo_terms / row_total
        prob_low = attn_prob.astype(jnp.bfloat16)
        d_prob = jnp.einsum("gbd,gsjd->gbsj", g_blk, v_sel, preferred_element_type=jnp.float32)
        row_delta = jnp.sum(attn_prob * d_prob, axis=(2, 3), keepdims=True)
        adjoint_weights = attn_prob * (d_prob - row_delta)
        temp_acc = temp_acc + jnp.sum(adjoint_weights * logit_matrix)
        adjoint_logits = (adjoint_weights * (channel_scale * reciprocal_sqrt_width)).astype(
            jnp.bfloat16
        )
        adjoint_probe = jnp.einsum(
            "gbsj,gsjd->gbd", adjoint_logits, k_sel, preferred_element_type=jnp.float32
        )
        d_keys = jnp.einsum(
            "gbsj,gbd->gsjd", adjoint_logits, q_blk, preferred_element_type=jnp.float32
        )
        d_values = jnp.einsum("gbsj,gbd->gsjd", prob_low, g_blk, preferred_element_type=jnp.float32)
        key_acc = key_acc.at[idx_blk].add(d_keys)
        value_acc = value_acc.at[idx_blk].add(d_values)
        return ((key_acc, value_acc, temp_acc), adjoint_probe.astype(jnp.bfloat16))

    start = (
        jnp.zeros((k_blocks, tile_span, channel_width), jnp.float32),
        jnp.zeros((k_blocks, tile_span, channel_width), jnp.float32),
        jnp.zeros((), jnp.float32),
    )
    (key_acc, value_acc, temp_acc), adjoint_probe = lax.scan(
        step, start, (q_groups, g_groups, i_groups, v_groups)
    )
    return (
        adjoint_probe.reshape(q_len, channel_width),
        key_acc.reshape(k_len, channel_width).astype(jnp.bfloat16),
        value_acc.reshape(k_len, channel_width).astype(jnp.bfloat16),
        temp_acc,
    )


def on_device(
    probe_tensor,
    matcher_tensor,
    payload_tensor,
    adjoint_attended,
    logit_scale,
    anchor_tiles,
    sampled_tiles,
):
    tok_local, seq_count, width = probe_tensor.shape
    channel_roster = logit_scale.shape[0]
    channel_width = width // channel_roster
    seq_parts = lax.axis_size("seq")
    item_total = seq_count * channel_roster
    copies = max(1, seq_parts // item_total)
    per_device = max(1, item_total // seq_parts)
    piece = tok_local // copies
    tile_index = min(TILE_SPAN, piece)

    def to_samples(array):
        return jnp.repeat(array.reshape(tok_local, item_total, channel_width), copies, axis=1)

    def to_shares(array):
        split = array.reshape(copies, piece, item_total, channel_width).transpose(1, 2, 0, 3)
        return split.reshape(piece, item_total * copies, channel_width)

    query_send = to_shares(probe_tensor)
    grad_send = to_shares(adjoint_attended)
    query_item = lax.all_to_all(query_send, "seq", split_axis=1, concat_axis=0, tiled=True)
    key_item = lax.all_to_all(
        to_samples(matcher_tensor), "seq", split_axis=1, concat_axis=0, tiled=True
    )
    value_item = lax.all_to_all(
        to_samples(payload_tensor), "seq", split_axis=1, concat_axis=0, tiled=True
    )
    grad_item = lax.all_to_all(grad_send, "seq", split_axis=1, concat_axis=0, tiled=True)
    length = key_item.shape[0]
    nblocks = length // TILE_SPAN
    my_index = lax.axis_index("seq")
    replica = my_index % copies
    position_pointer, position_usable = block_lists(anchor_tiles, sampled_tiles, nblocks)
    first_item = my_index // copies * per_device
    channel_finder = (first_item + jnp.arange(per_device, dtype=jnp.int32)) % channel_roster
    channel_subset = channel_finder[:, None] == jnp.arange(channel_roster, dtype=jnp.int32)[None, :]
    sample_scales = jnp.sum(jnp.where(channel_subset, logit_scale[None, :], 0.0), axis=1)
    item_index = jnp.sum(
        jnp.where(channel_subset[:, :, None, None], position_pointer[None], 0), axis=1
    )
    item_valid = jnp.any(channel_subset[:, :, None, None] & position_usable[None], axis=1)
    tiles_per_device = share_units(replica, tok_local, seq_parts, copies, tile_index, TILE_SPAN)
    item_index = jnp.take(item_index, tiles_per_device, axis=1)
    item_valid = jnp.take(item_valid, tiles_per_device, axis=1)

    def sample_mapped(sample_operands):
        (
            probe_vector,
            matcher_tiles,
            payload_tiles,
            adjoint_signal,
            channel_scale,
            sample_indices,
            sample_valid_mask,
        ) = sample_operands
        return attend_sample(
            probe_vector,
            matcher_tiles,
            payload_tiles,
            adjoint_signal,
            channel_scale,
            sample_indices,
            sample_valid_mask,
            tile_index,
            TILE_SPAN,
        )

    adjoint_probe, adjoint_matcher, adjoint_payload, adjoint_scale = lax.map(
        sample_mapped,
        (
            jnp.moveaxis(query_item, 1, 0),
            jnp.moveaxis(key_item, 1, 0),
            jnp.moveaxis(value_item, 1, 0),
            jnp.moveaxis(grad_item, 1, 0),
            sample_scales,
            item_index,
            item_valid,
        ),
    )
    scale_pieces = jnp.sum(jnp.where(channel_subset, adjoint_scale[:, None], 0.0), axis=0)
    adjoint_scales = lax.psum(scale_pieces, ("seq", "fsdp"))
    query_grad = jnp.moveaxis(adjoint_probe, 0, 1)
    key_send = jnp.moveaxis(adjoint_matcher, 0, 1)
    value_send = jnp.moveaxis(adjoint_payload, 0, 1)
    back_query = lax.all_to_all(query_grad, "seq", split_axis=0, concat_axis=1, tiled=True)
    returned_key = lax.all_to_all(key_send, "seq", split_axis=0, concat_axis=1, tiled=True)
    returned_value = lax.all_to_all(value_send, "seq", split_axis=0, concat_axis=1, tiled=True)

    def combine_portions(received):
        summed = jnp.sum(
            received.astype(jnp.float32).reshape(tok_local, item_total, copies, channel_width),
            axis=2,
        )
        return summed.astype(jnp.bfloat16).reshape(tok_local, seq_count, width)

    query_gradients = (
        back_query.reshape(piece, item_total, copies, channel_width)
        .transpose(2, 0, 1, 3)
        .reshape(tok_local, seq_count, width)
    )
    return (
        query_gradients,
        combine_portions(returned_key),
        combine_portions(returned_value),
        adjoint_scales,
    )


def solution(mesh):
    placed = (
        P("seq", "fsdp", None),
        P("seq", "fsdp", None),
        P("seq", "fsdp", None),
        P("seq", "fsdp", None),
        P(),
        P(),
        P(),
    )
    return jax.shard_map(
        on_device,
        mesh=mesh,
        in_specs=placed,
        out_specs=(P("seq", "fsdp", None), P("seq", "fsdp", None), P("seq", "fsdp", None), P()),
        check_vma=False,
    )
```

profile of v0, /device:TPU:0, one launch (start us, length us, event | category | flops | bytes accessed | tf_op | source)
XLA Modules:
  0.0 318.6 jit_solution(13504506956540045981)
XLA Ops:
  0.6 1.2 copy.69
  2.8 8.5 %all-to-all-start = ((bf16[128,16,128]{2,0,1:T(8,128)(2,1)}), bf16[128,16,128]{2,0,1:T(8,128)(2,1)}, u32[]{:S(2)}, u32[]{:S(2)}) async-start(bf16[128,16,128]{2,0,1:T(8,128)(2,1)} %copy.49), calls=%async_computation | async-start | bytes 1048576 | tf_op jit(solution)/shard_map/all_to_all | solution.py:152
  12.4 14.1 %all-to-all-done = bf16[128,16,128]{2,0,1:T(8,128)(2,1)} async-done(((bf16[128,16,128]{2,0,1:T(8,128)(2,1)}), bf16[128,16,128]{2,0,1:T(8,128)(2,1)}, u32[]{:S(2)}, u32[]{:S(2)}) %all-to-all-start) | async-done | bytes 524320 | tf_op jit(solution)/shard_map/all_to_all | solution.py:152
  26.5 4.2 %all-to-all-start.1 = ((bf16[128,16,128]{2,0,1:T(8,128)(2,1)}), bf16[128,16,128]{2,0,1:T(8,128)(2,1)}, u32[]{:S(2)}, u32[]{:S(2)}) async-start(bf16[128,16,128]{2,0,1:T(8,128)(2,1)} %copy.50), calls=%async_computation.1 | async-start | bytes 1048576 | tf_op jit(solution)/shard_map/all_to_all | solution.py:153
  31.8 13.1 %all-to-all-done.1 = bf16[128,16,128]{2,0,1:T(8,128)(2,1)} async-done(((bf16[128,16,128]{2,0,1:T(8,128)(2,1)}), bf16[128,16,128]{2,0,1:T(8,128)(2,1)}, u32[]{:S(2)}, u32[]{:S(2)}) %all-to-all-start.1) | async-done | bytes 524320 | tf_op jit(solution)/shard_map/all_to_all | solution.py:153
  44.9 4.2 %all-to-all-start.2 = ((bf16[128,16,128]{2,0,1:T(8,128)(2,1)}), bf16[128,16,128]{2,0,1:T(8,128)(2,1)}, u32[]{:S(2)}, u32[]{:S(2)}) async-start(bf16[128,16,128]{2,0,1:T(8,128)(2,1)} %copy.51), calls=%async_computation.2 | async-start | bytes 1048576 | tf_op jit(solution)/shard_map/all_to_all | solution.py:159
  50.8 12.2 %all-to-all-done.2 = bf16[128,16,128]{2,0,1:T(8,128)(2,1)} async-done(((bf16[128,16,128]{2,0,1:T(8,128)(2,1)}), bf16[128,16,128]{2,0,1:T(8,128)(2,1)}, u32[]{:S(2)}, u32[]{:S(2)}) %all-to-all-start.2) | async-done | bytes 524320 | tf_op jit(solution)/shard_map/all_to_all | solution.py:159
  63.0 4.2 %all-to-all-start.3 = ((bf16[128,16,128]{2,0,1:T(8,128)(2,1)}), bf16[128,16,128]{2,0,1:T(8,128)(2,1)}, u32[]{:S(2)}, u32[]{:S(2)}) async-start(bf16[128,16,128]{2,0,1:T(8,128)(2,1)} %copy.52), calls=%async_computation.3 | async-start | bytes 1048576 | tf_op jit(solution)/shard_map/all_to_all | solution.py:156
  70.1 10.7 %all-to-all-done.3 = bf16[128,16,128]{2,0,1:T(8,128)(2,1)} async-done(((bf16[128,16,128]{2,0,1:T(8,128)(2,1)}), bf16[128,16,128]{2,0,1:T(8,128)(2,1)}, u32[]{:S(2)}, u32[]{:S(2)}) %all-to-all-start.3) | async-done | bytes 524320 | tf_op jit(solution)/shard_map/all_to_all | solution.py:156
  80.8 1.1 broadcast.417
  81.9 1.1 broadcast.417.clone
  83.0 145.9 %while.32 = (s32[]{:T(128)}, f32[32,64,128]{2,1,0:T(8,128)}, f32[32,64,128]{2,1,0:T(8,128)}, f32[]{:T(128)}, bf16[4,8,64,128]{3,2,1,0:T(8,128)(2,1)}, /*index=5*...) while((s32[]{:T(128)}, f32[32,64,128]{2,1,0:T(8,128)}, ...), condition=%wide.region_10.11_spmd, body=%wide.region_3.10_spmd.sunk | while | flops 345308864 | bytes 46302156 | solution.py:113
  83.1 1.8 gather_fusion
  84.9 1.4 fusion.68
  86.9 3.0 fusion.71
  89.9 10.4 %scatter_fusion.1 = f32[32,64,128]{2,1,0:T(8,128)} fusion(f32[32,64,128]{2,1,0:T(8,128)} %get-tuple-element.357, s32[64]{0:T(128)S(1)} %reshape.483, f32[64,64,128]{2,1,0:T(8,128)} %bitcast.147), kind=kCustom, calls=%fused_computation.5.clone.1 | custom fusion | flops 524288 | bytes 6291712 | tf_op jit(solution)/shard_map/while/body/eval_jaxpr/while/body/eval_jaxpr/scatter-add | solution.py:105
  100.3 2.7 gather_fusion.1
  103.0 2.2 multiply_reduce_fusion.4
  105.1 1.8 multiply_reduce_fusion.5
  107.9 2.7 fusion.70
  110.6 7.0 %scatter_fusion = f32[32,64,128]{2,1,0:T(8,128)S(1)} fusion(f32[32,64,128]{2,1,0:T(8,128)S(1)} %copy-done.2, s32[64]{0:T(128)S(1)} %reshape.483, f32[64,64,128]{2,1,0:T(8,128)} %bitcast.146), kind=kCustom, calls=%fused_computation.4.clone.1 | custom fusion | flops 524288 | bytes 6291712 | tf_op jit(solution)/shard_map/while/body/eval_jaxpr/while/body/eval_jaxpr/scatter-add | solution.py:104
  117.7 1.1 fusion.72
  119.6 1.8 gather_fusion
  121.4 1.4 fusion.68
  123.4 3.0 fusion.71
  126.4 10.3 %scatter_fusion.1 = f32[32,64,128]{2,1,0:T(8,128)} fusion(f32[32,64,128]{2,1,0:T(8,128)} %get-tuple-element.357, s32[64]{0:T(128)S(1)} %reshape.483, f32[64,64,128]{2,1,0:T(8,128)} %bitcast.147), kind=kCustom, calls=%fused_computation.5.clone.1 | custom fusion | flops 524288 | bytes 6291712 | tf_op jit(solution)/shard_map/while/body/eval_jaxpr/while/body/eval_jaxpr/scatter-add | solution.py:105
  136.7 2.7 gather_fusion.1
  139.4 2.2 multiply_reduce_fusion.4
  141.6 1.8 multiply_reduce_fusion.5
  144.4 2.7 fusion.70
  147.1 7.0 %scatter_fusion = f32[32,64,128]{2,1,0:T(8,128)S(1)} fusion(f32[32,64,128]{2,1,0:T(8,128)S(1)} %copy-done.2, s32[64]{0:T(128)S(1)} %reshape.483, f32[64,64,128]{2,1,0:T(8,128)} %bitcast.146), kind=kCustom, calls=%fused_computation.4.clone.1 | custom fusion | flops 524288 | bytes 6291712 | tf_op jit(solution)/shard_map/while/body/eval_jaxpr/while/body/eval_jaxpr/scatter-add | solution.py:104
  154.2 1.1 fusion.72
  156.1 1.8 gather_fusion
  157.9 1.4 fusion.68
  159.9 3.0 fusion.71
  162.9 10.3 %scatter_fusion.1 = f32[32,64,128]{2,1,0:T(8,128)} fusion(f32[32,64,128]{2,1,0:T(8,128)} %get-tuple-element.357, s32[64]{0:T(128)S(1)} %reshape.483, f32[64,64,128]{2,1,0:T(8,128)} %bitcast.147), kind=kCustom, calls=%fused_computation.5.clone.1 | custom fusion | flops 524288 | bytes 6291712 | tf_op jit(solution)/shard_map/while/body/eval_jaxpr/while/body/eval_jaxpr/scatter-add | solution.py:105
  173.2 2.7 gather_fusion.1
  175.9 2.2 multiply_reduce_fusion.4
  178.1 1.8 multiply_reduce_fusion.5
  180.9 2.7 fusion.70
  183.6 7.0 %scatter_fusion = f32[32,64,128]{2,1,0:T(8,128)S(1)} fusion(f32[32,64,128]{2,1,0:T(8,128)S(1)} %copy-done.2, s32[64]{0:T(128)S(1)} %reshape.483, f32[64,64,128]{2,1,0:T(8,128)} %bitcast.146), kind=kCustom, calls=%fused_computation.4.clone.1 | custom fusion | flops 524288 | bytes 6291712 | tf_op jit(solution)/shard_map/while/body/eval_jaxpr/while/body/eval_jaxpr/scatter-add | solution.py:104
  190.7 1.1 fusion.72
  192.6 1.8 gather_fusion
  194.4 1.4 fusion.68
  196.4 3.0 fusion.71
  199.4 10.3 %scatter_fusion.1 = f32[32,64,128]{2,1,0:T(8,128)} fusion(f32[32,64,128]{2,1,0:T(8,128)} %get-tuple-element.357, s32[64]{0:T(128)S(1)} %reshape.483, f32[64,64,128]{2,1,0:T(8,128)} %bitcast.147), kind=kCustom, calls=%fused_computation.5.clone.1 | custom fusion | flops 524288 | bytes 6291712 | tf_op jit(solution)/shard_map/while/body/eval_jaxpr/while/body/eval_jaxpr/scatter-add | solution.py:105
  209.7 2.7 gather_fusion.1
  212.4 2.2 multiply_reduce_fusion.4
  214.6 1.8 multiply_reduce_fusion.5
  217.4 2.7 fusion.70
  220.1 7.0 %scatter_fusion = f32[32,64,128]{2,1,0:T(8,128)S(1)} fusion(f32[32,64,128]{2,1,0:T(8,128)S(1)} %copy-done.2, s32[64]{0:T(128)S(1)} %reshape.483, f32[64,64,128]{2,1,0:T(8,128)} %bitcast.146), kind=kCustom, calls=%fused_computation.4.clone.1 | custom fusion | flops 524288 | bytes 6291712 | tf_op jit(solution)/shard_map/while/body/eval_jaxpr/while/body/eval_jaxpr/scatter-add | solution.py:104
  227.2 1.1 fusion.72
  229.0 1.4 convert_element_type.88
  230.9 1.0 reduce.5
  232.8 3.8 %all-to-all-start.5 = ((bf16[16,2,8192]{2,1,0:T(2,128)(2,1)}), bf16[16,2,8192]{2,1,0:T(2,128)(2,1)S(1)}, u32[]{:S(2)}, u32[]{:S(2)}) async-start(bf16[16,2,8192]{2,1,0:T(2,128)(2,1)} %reshape.462), calls=%async_computation.5 | async-start | bytes 1048576 | tf_op jit(solution)/shard_map/all_to_all | solution.py:217
  236.7 1.1 reduce.6
  238.7 11.7 %all-to-all-done.5 = bf16[16,2,8192]{2,1,0:T(2,128)(2,1)S(1)} async-done(((bf16[16,2,8192]{2,1,0:T(2,128)(2,1)}), bf16[16,2,8192]{2,1,0:T(2,128)(2,1)S(1)}, u32[]{:S(2)}, u32[]{:S(2)}) %all-to-all-start.5) | async-done | bytes 524320 | tf_op jit(solution)/shard_map/all_to_all | solution.py:217
  250.4 3.8 %all-to-all-start.6 = ((bf16[16,2,8192]{2,1,0:T(2,128)(2,1)}), bf16[16,2,8192]{2,1,0:T(2,128)(2,1)S(1)}, u32[]{:S(2)}, u32[]{:S(2)}) async-start(bf16[16,2,8192]{2,1,0:T(2,128)(2,1)} %reshape.464), calls=%async_computation.6 | async-start | bytes 1048576 | tf_op jit(solution)/shard_map/all_to_all | solution.py:218
  254.2 1.0 reduce.4
  256.2 11.7 %all-to-all-done.6 = bf16[16,2,8192]{2,1,0:T(2,128)(2,1)S(1)} async-done(((bf16[16,2,8192]{2,1,0:T(2,128)(2,1)}), bf16[16,2,8192]{2,1,0:T(2,128)(2,1)S(1)}, u32[]{:S(2)}, u32[]{:S(2)}) %all-to-all-start.6) | async-done | bytes 524320 | tf_op jit(solution)/shard_map/all_to_all | solution.py:218
  267.9 3.8 %all-to-all-start.4 = ((bf16[16,2,8192]{2,1,0:T(2,128)(2,1)}), bf16[16,2,8192]{2,1,0:T(2,128)(2,1)S(1)}, u32[]{:S(2)}, u32[]{:S(2)}) async-start(bf16[16,2,8192]{2,1,0:T(2,128)(2,1)} %reshape.460), calls=%async_computation.4 | async-start | bytes 1048576 | tf_op jit(solution)/shard_map/all_to_all | solution.py:216
  271.8 41.1 %psum.7 = f32[16]{0:T(128)} all-reduce(f32[16]{0:T(128)S(1)} %broadcast_select_fusion), channel_id=1, replica_groups=mesh['seq'=16,'fsdp'=2] {'seq','fsdp'}, use_global_device_ids=true, to_apply=%region_11.12 | all-reduce | flops 16 | bytes 128 | tf_op jit(solution)/shard_map/psum | solution.py:212
  313.8 1.0 copy.60
  315.7 1.0 copy.61
  (116 shorter events, 20.8 us)
Async XLA Ops:
  0.6 10.7 %copy-start.5 = (bf16[128,1,2048]{2,0,1:T(8,128)(2,1)S(1)}, bf16[128,1,2048]{2,0,1:T(8,128)(2,1)}, u32[]{:S(2)}) copy-start(bf16[128,1,2048]{2,0,1:T(8,128)(2,1)} %param.11) | copy-start | bytes 1572868
  2.8 27.9 %copy-start.6 = (bf16[128,1,2048]{2,0,1:T(8,128)(2,1)S(1)}, bf16[128,1,2048]{2,0,1:T(8,128)(2,1)}, u32[]{:S(2)}) copy-start(bf16[128,1,2048]{2,0,1:T(8,128)(2,1)} %param.13) | copy-start | bytes 1572868
  2.8 23.7 %all-to-all-start = ((bf16[128,16,128]{2,0,1:T(8,128)(2,1)}), bf16[128,16,128]{2,0,1:T(8,128)(2,1)}, u32[]{:S(2)}, u32[]{:S(2)}) async-start(bf16[128,16,128]{2,0,1:T(8,128)(2,1)} %copy.49), calls=%async_computation | async-start | bytes 1048576 | tf_op jit(solution)/shard_map/all_to_all | solution.py:152
  12.4 36.8 %copy-start.11 = (s32[3]{0:T(128)S(1)}, s32[3]{0:T(128)}, u32[]{:S(2)}) copy-start(s32[3]{0:T(128)} %constant.219.clone) | copy-start | bytes 40
  12.4 36.9 %copy-start.10 = (s32[16,2]{0,1:T(2,128)S(1)}, s32[16,2]{0,1:T(2,128)}, u32[]{:S(2)}) copy-start(s32[16,2]{0,1:T(2,128)} %param.15) | copy-start | bytes 388
  12.4 37.0 %copy-start.9 = (s32[16,32,3]{1,0,2:T(8,128)S(1)}, s32[16,32,3]{1,0,2:T(8,128)}, u32[]{:S(2)}) copy-start(s32[16,32,3]{1,0,2:T(8,128)} %param.16) | copy-start | bytes 18436
  12.4 37.2 %copy-start.7 = (bf16[128,1,2048]{2,0,1:T(8,128)(2,1)S(1)}, bf16[128,1,2048]{2,0,1:T(8,128)(2,1)}, u32[]{:S(2)}) copy-start(bf16[128,1,2048]{2,0,1:T(8,128)(2,1)} %param.12) | copy-start | bytes 1572868
  26.5 18.4 %all-to-all-start.1 = ((bf16[128,16,128]{2,0,1:T(8,128)(2,1)}), bf16[128,16,128]{2,0,1:T(8,128)(2,1)}, u32[]{:S(2)}, u32[]{:S(2)}) async-start(bf16[128,16,128]{2,0,1:T(8,128)(2,1)} %copy.50), calls=%async_computation.1 | async-start | bytes 1048576 | tf_op jit(solution)/shard_map/all_to_all | solution.py:153
  31.8 36.9 %copy-start.12 = (f32[16]{0:T(128)S(1)}, f32[16]{0:T(128)}, u32[]{:S(2)}) copy-start(f32[16]{0:T(128)} %param.14) | copy-start | bytes 196
  44.9 18.1 %all-to-all-start.2 = ((bf16[128,16,128]{2,0,1:T(8,128)(2,1)}), bf16[128,16,128]{2,0,1:T(8,128)(2,1)}, u32[]{:S(2)}, u32[]{:S(2)}) async-start(bf16[128,16,128]{2,0,1:T(8,128)(2,1)} %copy.51), calls=%async_computation.2 | async-start | bytes 1048576 | tf_op jit(solution)/shard_map/all_to_all | solution.py:159
  63.0 17.8 %all-to-all-start.3 = ((bf16[128,16,128]{2,0,1:T(8,128)(2,1)}), bf16[128,16,128]{2,0,1:T(8,128)(2,1)}, u32[]{:S(2)}, u32[]{:S(2)}) async-start(bf16[128,16,128]{2,0,1:T(8,128)(2,1)} %copy.52), calls=%async_computation.3 | async-start | bytes 1048576 | tf_op jit(solution)/shard_map/all_to_all | solution.py:156
  107.0 1.0 copy-start
  107.0 3.6 %copy-start.2 = (f32[32,64,128]{2,1,0:T(8,128)S(1)}, f32[32,64,128]{2,1,0:T(8,128)}, u32[]{:S(2)}) copy-start(f32[32,64,128]{2,1,0:T(8,128)} %get-tuple-element.356) | copy-start | bytes 3145732 | tf_op jit(solution)/shard_map/while/body/eval_jaxpr/while
  110.6 7.0 %copy-start.1 = (bf16[8,64,8,64]{1,3,2,0:T(8,128)(2,1)S(1)}, bf16[8,64,8,64]{1,3,2,0:T(8,128)(2,1)}, u32[]{:S(2)}) copy-start(bf16[8,64,8,64]{1,3,2,0:T(8,128)(2,1)} %copy-done) | copy-start | bytes 1572868 | tf_op jit(solution)/shard_map/while/body/eval_jaxpr/while
  117.7 1.8 copy-start.3
  143.5 1.0 copy-start
  143.5 3.6 %copy-start.2 = (f32[32,64,128]{2,1,0:T(8,128)S(1)}, f32[32,64,128]{2,1,0:T(8,128)}, u32[]{:S(2)}) copy-start(f32[32,64,128]{2,1,0:T(8,128)} %get-tuple-element.356) | copy-start | bytes 3145732 | tf_op jit(solution)/shard_map/while/body/eval_jaxpr/while
  147.1 7.1 %copy-start.1 = (bf16[8,64,8,64]{1,3,2,0:T(8,128)(2,1)S(1)}, bf16[8,64,8,64]{1,3,2,0:T(8,128)(2,1)}, u32[]{:S(2)}) copy-start(bf16[8,64,8,64]{1,3,2,0:T(8,128)(2,1)} %copy-done) | copy-start | bytes 1572868 | tf_op jit(solution)/shard_map/while/body/eval_jaxpr/while
  154.1 1.8 copy-start.3
  179.9 1.0 copy-start
  180.0 3.6 %copy-start.2 = (f32[32,64,128]{2,1,0:T(8,128)S(1)}, f32[32,64,128]{2,1,0:T(8,128)}, u32[]{:S(2)}) copy-start(f32[32,64,128]{2,1,0:T(8,128)} %get-tuple-element.356) | copy-start | bytes 3145732 | tf_op jit(solution)/shard_map/while/body/eval_jaxpr/while
  183.6 7.1 %copy-start.1 = (bf16[8,64,8,64]{1,3,2,0:T(8,128)(2,1)S(1)}, bf16[8,64,8,64]{1,3,2,0:T(8,128)(2,1)}, u32[]{:S(2)}) copy-start(bf16[8,64,8,64]{1,3,2,0:T(8,128)(2,1)} %copy-done) | copy-start | bytes 1572868 | tf_op jit(solution)/shard_map/while/body/eval_jaxpr/while
  190.6 1.8 copy-start.3
  216.4 1.0 copy-start
  216.4 3.6 %copy-start.2 = (f32[32,64,128]{2,1,0:T(8,128)S(1)}, f32[32,64,128]{2,1,0:T(8,128)}, u32[]{:S(2)}) copy-start(f32[32,64,128]{2,1,0:T(8,128)} %get-tuple-element.356) | copy-start | bytes 3145732 | tf_op jit(solution)/shard_map/while/body/eval_jaxpr/while
  220.1 7.1 %copy-start.1 = (bf16[8,64,8,64]{1,3,2,0:T(8,128)(2,1)S(1)}, bf16[8,64,8,64]{1,3,2,0:T(8,128)(2,1)}, u32[]{:S(2)}) copy-start(bf16[8,64,8,64]{1,3,2,0:T(8,128)(2,1)} %copy-done) | copy-start | bytes 1572868 | tf_op jit(solution)/shard_map/while/body/eval_jaxpr/while
  227.1 1.8 copy-start.3
  229.0 7.6 %copy-start.4 = (f32[32,64,128]{2,1,0:T(8,128)S(1)}, f32[32,64,128]{2,1,0:T(8,128)}, u32[]{:S(2)}) copy-start(f32[32,64,128]{2,1,0:T(8,128)} %get-tuple-element.213) | copy-start | bytes 3145732
  232.8 17.6 %all-to-all-start.5 = ((bf16[16,2,8192]{2,1,0:T(2,128)(2,1)}), bf16[16,2,8192]{2,1,0:T(2,128)(2,1)S(1)}, u32[]{:S(2)}, u32[]{:S(2)}) async-start(bf16[16,2,8192]{2,1,0:T(2,128)(2,1)} %reshape.462), calls=%async_computation.5 | async-start | bytes 1048576 | tf_op jit(solution)/shard_map/all_to_all | solution.py:217
  236.6 17.6 %copy-start.8 = (bf16[4,8,64,128]{3,2,1,0:T(8,128)(2,1)S(1)}, bf16[4,8,64,128]{3,2,1,0:T(8,128)(2,1)}, u32[]{:S(2)}) copy-start(bf16[4,8,64,128]{3,2,1,0:T(8,128)(2,1)} %get-tuple-element.211) | copy-start | bytes 1572868
  250.4 17.5 %all-to-all-start.6 = ((bf16[16,2,8192]{2,1,0:T(2,128)(2,1)}), bf16[16,2,8192]{2,1,0:T(2,128)(2,1)S(1)}, u32[]{:S(2)}, u32[]{:S(2)}) async-start(bf16[16,2,8192]{2,1,0:T(2,128)(2,1)} %reshape.464), calls=%async_computation.6 | async-start | bytes 1048576 | tf_op jit(solution)/shard_map/all_to_all | solution.py:218
  267.9 48.8 %all-to-all-start.4 = ((bf16[16,2,8192]{2,1,0:T(2,128)(2,1)}), bf16[16,2,8192]{2,1,0:T(2,128)(2,1)S(1)}, u32[]{:S(2)}, u32[]{:S(2)}) async-start(bf16[16,2,8192]{2,1,0:T(2,128)(2,1)} %reshape.460), calls=%async_computation.4 | async-start | bytes 1048576 | tf_op jit(solution)/shard_map/all_to_all | solution.py:216
where the time goes:
time: 321 us; the launch traced here: 319 us
  other arithmetic  85.4 us (27%)
  waiting for transfers between devices  73.5 us (23%)
  matrix products  41.1 us (13%)
  blocking collectives  41.1 us (13%)
  local copies, waits for them, and re-layouts  40.2 us (13%)
  starting transfers between devices  32.7 us (10%)
    scatter-add x4, other arithmetic, step(): value_acc = value_acc.at[idx_blk].add(d_values)  41.3 us
    psum x1, blocking collectives, on_device(): adjoint_scales = lax.psum(scale_pieces, ('seq', 'fsdp'))  41.1 us
    scatter-add x4, other arithmetic, step(): key_acc = key_acc.at[idx_blk].add(d_keys)  28.1 us
    all_to_all x1, waiting for transfers between devices, on_device(): lax.all_to_all(query_send, 'seq', split_axis=1, concat_axis=0, tiled=True)  14.1 us
    all_to_all x1, waiting for transfers between devices, on_device(): lax.all_to_all(to_samples(matcher_tensor), 'seq', split_axis=1, concat_ax...  13.1 us
    all_to_all x1, waiting for transfers between devices, on_device(): lax.all_to_all(grad_send, 'seq', split_axis=1, concat_axis=0, tiled=True)  12.2 us
    dot_general x4, matrix products, step(): jnp.einsum('gbsj,gbd->gsjd', prob_low, g_blk, preferred_element_type=jnp....  11.9 us
    all_to_all x1, waiting for transfers between devices, on_device(): lax.all_to_all(value_send, 'seq', split_axis=0, concat_axis=1, tiled=True)  11.7 us
  transfers between devices with their start and end apart: 7, of which 6 were waited for; matrix products, arithmetic and copies ran while one was open for 4% of the time, Pallas kernels for 0%

commit v1 on v0

v1 whole, which is shorter than its diff:
```python
import functools
import math

import jax
import jax.numpy as jnp
from jax import lax
from jax.experimental import pallas as pl
from jax.experimental.pallas import tpu as pltpu
from jax.sharding import PartitionSpec as P

TILE_SPAN = 64
MASKED = -1e30
MESH = pl.DeviceIdType.MESH
F32 = jnp.float32
BF16 = jnp.bfloat16


def attention_kernel(
    dims,
    q_in,
    k_in,
    v_in,
    g_in,
    scale_in,
    table,
    q_out,
    k_out,
    v_out,
    scale_out,
    qbuf,
    kbuf,
    vbuf,
    gbuf,
    s_ref,
    p_ref,
    dk_acc,
    dv_acc,
    dk_anchor,
    dv_anchor,
    dk_chain,
    dv_chain,
    dq_send,
    dk_send,
    dv_send,
    temp_acc,
    pair_terms,
    item_terms,
    in_send,
    in_recv,
    out_send,
    out_recv,
    term_send,
    term_recv,
):
    n, nf, copies, tok, piece, tile, width, heads, n_anchor, n_random = dims
    span = TILE_SPAN
    nblocks = n * tok // span
    units = piece // tile
    entries = n * units * n_random
    window = 3 * span
    reciprocal = 1.0 / math.sqrt(width)
    me = lax.axis_index("seq")
    mine = lax.axis_index("fsdp")
    item = me // copies
    replica = me % copies
    cols = lambda d: pl.ds(pl.multiple_of(d // copies * width, width), width)

    barrier = pltpu.get_barrier_semaphore()

    def greet(o, _):
        pl.semaphore_signal(
            barrier, inc=1, device_id={"seq": (me + o) % n}, device_id_type=MESH
        )
        return _

    lax.fori_loop(1, n, greet, 0)
    for o in range(1, nf):
        pl.semaphore_signal(
            barrier, inc=1, device_id={"fsdp": (mine + o) % nf}, device_id_type=MESH
        )
    pl.semaphore_wait(barrier, n - 1 + nf - 1)

    arrivals = (
        (k_in, kbuf, tok // span, 1),
        (q_in, qbuf, piece, 0),
        (g_in, gbuf, piece, 0),
        (v_in, vbuf, tok // span, 1),
    )
    for a, (source, target, rows, shift) in enumerate(arrivals):

        def block(d):
            if shift:
                return source.at[:, :, cols(d)]
            return source.at[pl.ds(pl.multiple_of(d % copies * rows, rows), rows), cols(d)]

        if shift:
            landing = target.at[pl.ds(shift + me * rows, rows)]
        else:
            landing = target.at[pl.ds(pl.multiple_of(me * rows, rows), rows)]

        def send(o, _):
            d = (me + o) % n
            pltpu.make_async_remote_copy(
                src_ref=block(d),
                dst_ref=landing,
                send_sem=in_send.at[a],
                recv_sem=in_recv.at[a],
                device_id={"seq": d},
                device_id_type=MESH,
            ).start()
            return _

        pltpu.make_async_copy(block(me), landing, in_recv.at[a]).start()
        lax.fori_loop(1, n, send, 0)

    def arrive(a):
        _, target, rows, shift = arrivals[a]
        ref = target.at[pl.ds(shift, n * rows)]
        pltpu.make_async_copy(ref, ref, in_recv.at[a]).wait()

    zero_block = jnp.zeros((span, width), BF16)
    for buf in (kbuf, vbuf):
        buf[0] = zero_block
        buf[nblocks + 1] = zero_block

    def clear(c, _):
        dk_acc[c] = jnp.zeros((span, width), F32)
        dv_acc[c] = jnp.zeros((span, width), F32)
        return _

    lax.fori_loop(0, nblocks + 2, clear, 0)
    dk_anchor[...] = jnp.zeros_like(dk_anchor)
    dv_anchor[...] = jnp.zeros_like(dv_anchor)
    dk_chain[0] = jnp.zeros((span, width), F32)
    dv_chain[0] = jnp.zeros((span, width), F32)
    temp_acc[...] = jnp.zeros_like(temp_acc)

    scale = scale_in[item % heads]
    alpha = scale * reciprocal
    anchors = [table[2 * entries + nblocks + x] for x in range(n_anchor)]
    slots = 3 + n_anchor + n_random
    slot_of = lax.broadcasted_iota(jnp.int32, (1, slots * span), 1) // span

    def unit_at(k, j):
        p = (me + 1 + k) % n
        row = pl.multiple_of(p * piece + j * tile, tile)
        blk = (p * tok + replica * piece + j * tile) // span
        return pl.ds(row, tile), blk, k * units + j

    def select(buf, blk, t):
        parts = [buf[pl.ds(blk, 3)].reshape(window, width)]
        for a in anchors:
            parts.append(buf[a + 1])
        for x in range(n_random):
            parts.append(buf[table[t * n_random + x] + 1])
        return jnp.concatenate(parts, axis=0)

    def bias_of(blk):
        off = lambda dead: jnp.where(dead, MASKED, 0.0).astype(F32)
        bias = jnp.where(slot_of == 0, off(blk == 0), 0.0)
        bias = jnp.where(slot_of == 2, off(blk == nblocks - 1), bias)
        for x, a in enumerate(anchors):
            bias = jnp.where(slot_of == 3 + x, off(jnp.abs(a - blk) <= 1), bias)
        return bias

    def scatter(got, places, acc, anchor, chain):
        base = window + n_anchor * span
        for (blk, t), d in zip(places, got):
            acc[pl.ds(blk, 3)] += d[:window].reshape(3, span, width)
            anchor[...] += d[window:base].reshape(n_anchor, span, width)
            for x in range(n_random):
                e = t * n_random + x
                before = table[entries + e]
                chain[e + 1] = chain[before] + d[base + x * span : base + (x + 1) * span]

    rows_by_cols = (((1,), (1,)), ((), ()))
    over_rows = (((0,), (0,)), ((), ()))

    arrive(0)
    arrive(1)

    def scores(k, _):
        for j in range(units):
            at, blk, t = unit_at(k, j)
            s = lax.dot_general(
                qbuf[at, :], select(kbuf, blk, t), rows_by_cols, preferred_element_type=F32
            )
            logits = s * alpha + bias_of(blk)
            e = jnp.exp(logits - jnp.max(logits, axis=1, keepdims=True))
            s_ref[at, :] = s
            p_ref[at, :] = e * (1.0 / jnp.sum(e, axis=1, keepdims=True))
        return _

    lax.fori_loop(0, n, scores, 0)

    arrive(2)

    def value_terms(k, _):
        got, places = [], []
        for j in range(units):
            at, blk, t = unit_at(k, j)
            low = p_ref[at, :].astype(BF16)
            got.append(
                lax.dot_general(low, gbuf[at, :], over_rows, preferred_element_type=F32)
            )
            places.append((blk, t))
        scatter(got, places, dv_acc, dv_anchor, dv_chain)
        return _

    lax.fori_loop(0, n, value_terms, 0)

    def send_back(source, rows, target, target_rows, x, k):
        d = (me + 1 + k) % n
        block = source.at[pl.ds(pl.multiple_of(d * rows, rows), rows)]

        @pl.when(k < n - 1)
        def _():
            pltpu.make_async_remote_copy(
                src_ref=block,
                dst_ref=target.at[target_rows, landing_cols[x]],
                send_sem=out_send.at[x],
                recv_sem=out_recv.at[x],
                device_id={"seq": d},
                device_id_type=MESH,
            ).start()

        @pl.when(k == n - 1)
        def _():
            pltpu.make_async_copy(
                source.at[pl.ds(pl.multiple_of(me * rows, rows), rows)],
                target.at[target_rows, landing_cols[x]],
                out_recv.at[x],
            ).start()

    own_part = pl.ds(pl.multiple_of(me * width, width), width)
    landing_cols = (cols(me), own_part, own_part)

    def finish(acc, anchor, chain, source, target, x):
        def step(k, _):
            d = (me + 1 + k) % n
            for b in range(tok // span):
                c = d * (tok // span) + b
                last = table[2 * entries + c]
                total = acc[c + 1] + chain[last]
                for y, a in enumerate(anchors):
                    total += jnp.where(a == c, anchor[y], 0.0)
                source[pl.ds(pl.multiple_of(c * span, span), span), :] = total.astype(BF16)
            send_back(source, tok, target, slice(None), x, k)
            return _

        lax.fori_loop(0, n, step, 0)

    finish(dv_acc, dv_anchor, dv_chain, dv_send, v_out, 2)

    arrive(3)

    def score_terms(k, _):
        got, places = [], []
        for j in range(units):
            at, blk, t = unit_at(k, j)
            dprob = lax.dot_general(
                gbuf[at, :], select(vbuf, blk, t), rows_by_cols, preferred_element_type=F32
            )
            prob = p_ref[at, :]
            delta = jnp.sum(prob * dprob, axis=1, keepdims=True)
            dscore = prob * (dprob - delta)
            both = dscore * s_ref[at, :]
            lanes = both[:, :width]
            for y in range(1, slots * span // width):
                lanes += both[:, y * width : (y + 1) * width]
            part = lanes[0:8]
            for y in range(1, tile // 8):
                part += lanes[y * 8 : (y + 1) * 8]
            temp_acc[...] += part
            draw = (dscore * alpha).astype(BF16)
            dq = jnp.dot(draw, select(kbuf, blk, t), preferred_element_type=F32)
            dq_send[at, :] = dq.astype(BF16)
            got.append(
                lax.dot_general(draw, qbuf[at, :], over_rows, preferred_element_type=F32)
            )
            places.append((blk, t))
        mine_rows = pl.ds(pl.multiple_of(replica * piece, piece), piece)
        send_back(dq_send, piece, q_out, mine_rows, 0, k)
        scatter(got, places, dk_acc, dk_anchor, dk_chain)
        return _

    lax.fori_loop(0, n, score_terms, 0)
    finish(dk_acc, dk_anchor, dk_chain, dk_send, k_out, 1)

    total = jnp.sum(temp_acc[...], axis=1, keepdims=True)
    total = jnp.sum(total, axis=0, keepdims=True) * reciprocal
    pair_terms[mine] = jnp.broadcast_to(total, (8, 128))
    for o in range(1, nf):
        pltpu.make_async_remote_copy(
            src_ref=pair_terms.at[mine],
            dst_ref=pair_terms.at[mine],
            send_sem=term_send.at[0],
            recv_sem=term_recv.at[0],
            device_id={"fsdp": (mine + o) % nf},
            device_id_type=MESH,
        ).start()
    rest = pair_terms.at[pl.ds(0, nf - 1)]
    pltpu.make_async_copy(rest, rest, term_recv.at[0]).wait()
    pltpu.make_async_copy(rest, rest, term_send.at[0]).wait()
    total = pair_terms[0]
    for o in range(1, nf):
        total += pair_terms[o]
    item_terms[me] = total

    def tell(o, _):
        pltpu.make_async_remote_copy(
            src_ref=item_terms.at[me],
            dst_ref=item_terms.at[me],
            send_sem=term_send.at[1],
            recv_sem=term_recv.at[1],
            device_id={"seq": (me + o) % n},
            device_id_type=MESH,
        ).start()
        return _

    lax.fori_loop(1, n, tell, 0)
    rest = item_terms.at[pl.ds(0, n - 1)]
    pltpu.make_async_copy(rest, rest, term_recv.at[1]).wait()
    pltpu.make_async_copy(rest, rest, term_send.at[1]).wait()
    lane = lax.broadcasted_iota(jnp.int32, (8, 128), 1)
    result = jnp.zeros((8, 128), F32)
    for d in range(n):
        result += jnp.where(lane == d // copies % heads, item_terms[d], 0.0)
    scale_out[...] = result

    for a, (_, target, rows, _) in enumerate(arrivals):
        ref = target.at[pl.ds(0, (n - 1) * rows)]
        pltpu.make_async_copy(ref, ref, in_send.at[a]).wait()
    for x, (source, rows, target) in enumerate(
        ((dq_send, piece, q_out), (dk_send, tok, k_out), (dv_send, tok, v_out))
    ):
        ref = source.at[pl.ds(0, (n - 1) * rows)]
        pltpu.make_async_copy(ref, ref, out_send.at[x]).wait()
        pltpu.make_async_copy(target, target, out_recv.at[x]).wait()


def slot_table(anchor_tiles, sampled_tiles, head, blocks, nblocks):
    tiles = jnp.take(lax.dynamic_index_in_dim(sampled_tiles, head, 0, False), blocks, axis=0)
    tiles = tiles.reshape(-1).astype(jnp.int32)
    place = jnp.arange(tiles.shape[0], dtype=jnp.int32)
    earlier = (tiles[:, None] == tiles[None, :]) & (place[None, :] < place[:, None])
    before = jnp.max(jnp.where(earlier, place[None, :] + 1, 0), axis=1)
    ids = jnp.arange(nblocks, dtype=jnp.int32)
    last = jnp.max(jnp.where(tiles[None, :] == ids[:, None], place[None, :] + 1, 0), axis=1)
    anchors = lax.dynamic_index_in_dim(anchor_tiles, head, 0, False).astype(jnp.int32)
    return jnp.concatenate([tiles, before, last, anchors])


def on_device(n, nf, probe, matcher, payload, adjoint, logit_scale, anchor_tiles, sampled_tiles):
    tok, seq_count, total_width = probe.shape
    heads = logit_scale.shape[0]
    width = total_width // heads
    copies = n // (seq_count * heads)
    assert seq_count == 1 and copies * heads == n
    piece = tok // copies
    tile = min(TILE_SPAN, piece)
    units = piece // tile
    n_anchor, n_random = anchor_tiles.shape[1], sampled_tiles.shape[2]
    nblocks = n * tok // TILE_SPAN
    me = lax.axis_index("seq")
    order = jnp.arange(n * units, dtype=jnp.int32)
    peer = (me + 1 + order // units) % n
    blocks = (peer * tok + me % copies * piece + order % units * tile) // TILE_SPAN
    table = slot_table(anchor_tiles, sampled_tiles, me // copies % heads, blocks, nblocks)

    dims = (n, nf, copies, tok, piece, tile, width, heads, n_anchor, n_random)
    keys = n * tok
    queries = n * piece
    slots = (3 + n_anchor + n_random) * TILE_SPAN
    chain = (n * units * n_random + 1, TILE_SPAN, width)
    padded = (nblocks + 2, TILE_SPAN, width)
    anywhere = pl.BlockSpec(memory_space=pl.ANY)
    scalars = pl.BlockSpec(memory_space=pltpu.SMEM)
    flat = lambda array: array.reshape(tok, total_width)
    tiled = lambda array: array.reshape(tok // TILE_SPAN, TILE_SPAN, total_width)
    parts = jax.ShapeDtypeStruct((tok, n * width), BF16)
    q_out, k_out, v_out, scales = pl.pallas_call(
        functools.partial(attention_kernel, dims),
        out_shape=(
            jax.ShapeDtypeStruct((tok, total_width), BF16),
            parts,
            parts,
            jax.ShapeDtypeStruct((8, 128), F32),
        ),
        in_specs=[anywhere] * 4 + [scalars] * 2,
        out_specs=(anywhere, anywhere, anywhere, pl.BlockSpec(memory_space=pltpu.VMEM)),
        scratch_shapes=[
            pltpu.VMEM((queries, width), BF16),
            pltpu.VMEM(padded, BF16),
            pltpu.VMEM(padded, BF16),
            pltpu.VMEM((queries, width), BF16),
            pltpu.VMEM((queries, slots), F32),
            pltpu.VMEM((queries, slots), F32),
            pltpu.VMEM(padded, F32),
            pltpu.VMEM(padded, F32),
            pltpu.VMEM((n_anchor, TILE_SPAN, width), F32),
            pltpu.VMEM((n_anchor, TILE_SPAN, width), F32),
            pltpu.VMEM(chain, F32),
            pltpu.VMEM(chain, F32),
            pltpu.VMEM((queries, width), BF16),
            pltpu.VMEM((keys, width), BF16),
            pltpu.VMEM((keys, width), BF16),
            pltpu.VMEM((8, 128), F32),
            pltpu.VMEM((nf, 8, 128), F32),
            pltpu.VMEM((n, 8, 128), F32),
            pltpu.SemaphoreType.DMA((4,)),
            pltpu.SemaphoreType.DMA((4,)),
            pltpu.SemaphoreType.DMA((3,)),
            pltpu.SemaphoreType.DMA((3,)),
            pltpu.SemaphoreType.DMA((2,)),
            pltpu.SemaphoreType.DMA((2,)),
        ],
        compiler_params=pltpu.CompilerParams(
            collective_id=0, has_side_effects=True, vmem_limit_bytes=56 * 1024 * 1024
        ),
        cost_estimate=pl.CostEstimate(
            flops=10 * queries * slots * width,
            bytes_accessed=14 * tok * total_width,
            transcendentals=queries * slots,
        ),
    )(flat(probe), tiled(matcher), tiled(payload), flat(adjoint), logit_scale, table)

    def combine(received):
        if copies > 1:
            pieces = received.astype(F32).reshape(tok, heads, copies, width)
            received = jnp.sum(pieces, axis=2).astype(BF16)
        return received.reshape(tok, seq_count, total_width)

    return q_out.reshape(probe.shape), combine(k_out), combine(v_out), scales[0, :heads]


def solution(mesh):
    placed = P("seq", "fsdp", None)
    return jax.shard_map(
        functools.partial(on_device, mesh.shape["seq"], mesh.shape["fsdp"]),
        mesh=mesh,
        in_specs=(placed, placed, placed, placed, P(), P(), P()),
        out_specs=(placed, placed, placed, P()),
        check_vma=False,
    )
```

time: 321 us -> 98.6 us (0.31)
  Pallas kernels: 0 us -> 89.7 us
  other arithmetic: 85.4 us -> 1.08 us
  waiting for transfers between devices: 73.5 us -> 0 us
  matrix products: 41.1 us -> 0 us
  blocking collectives: 41.1 us -> 0 us
  local copies, waits for them, and re-layouts: 40.2 us -> 6.78 us
  starting transfers between devices: 32.7 us -> 0 us
    pallas_call x0 -> x1, Pallas kernels: none -> 89.7 us  [on_device(): pl.pallas_call(functools.partial(attention_kernel, dims), out_shape=(jax....]
    all_to_all x7 -> x0, waiting for transfers between devices: 73.5 us -> none  [the longest x1 14.1 us: on_device(): lax.all_to_all(query_send, 'seq', split_axis=1, concat_axis=0, tiled=True)]
    scatter-add x8 -> x0, other arithmetic: 69.5 us -> none  [the longest x4 41.3 us: step(): value_acc = value_acc.at[idx_blk].add(d_values)]
    dot_general x20 -> x0, matrix products: 41.1 us -> none  [the longest x4 11.9 us: step(): jnp.einsum('gbsj,gbd->gsjd', prob_low, g_blk, preferred_element_type=jnp....]
    psum x1 -> x0, blocking collectives: 41.1 us -> none  [on_device(): adjoint_scales = lax.psum(scale_pieces, ('seq', 'fsdp'))]
    all_to_all x7 -> x0, starting transfers between devices: 32.7 us -> none  [the longest x1 8.5 us: on_device(): lax.all_to_all(query_send, 'seq', split_axis=1, concat_axis=0, tiled=True)]
    gather x10 -> x1, local copies, waits for them, and re-layouts: 19.2 us -> 0.57 us  [slot_table(): jnp.take(lax.dynamic_index_in_dim(sampled_tiles, head, 0, False), blocks,...]
    reduce_sum x10 -> x0, other arithmetic: 10.7 us -> none  [the longest x4 7.36 us: step(): temp_acc = temp_acc + jnp.sum(adjoint_weights * logit_matrix)]
  transfers between devices with their start and end apart: 7 -> 0, of which waited for: 6 -> 0; matrix products, arithmetic and copies ran while one was open for 4% -> 0% of each run, Pallas kernels for 0% -> 0%
where the time goes in v1:
time: 98.6 us; the launch traced here: 98.3 us
  Pallas kernels  89.7 us (91%)
  local copies, waits for them, and re-layouts  6.78 us (7%)
  other arithmetic  1.08 us (1%)
    pallas_call x1, Pallas kernels, on_device(): pl.pallas_call(functools.partial(attention_kernel, dims), out_shape=(jax....  89.7 us
    unnamed x11, local copies, waits for them, and re-layouts  4.64 us

profile of v1, /device:TPU:0, one launch (start us, length us, event | category | flops | bytes accessed | tf_op | source)
XLA Modules:
  0.0 98.3 jit_solution(17933475253155231618)
XLA Ops:
  0.6 0.0 copy-start
  0.7 0.0 copy-start.3
  0.7 0.7 copy-done.3
  1.3 0.2 dynamic-slice_reduce_fusion
  1.6 0.0 copy-done
  1.6 0.1 copy.14
  1.7 0.6 gather_fusion
  2.3 0.1 broadcast_select_fusion
  2.4 0.1 select_n.131
  2.5 0.1 select_reduce_fusion.1
  2.6 0.2 select_reduce_fusion
  2.8 0.6 pad_add_fusion.table
  3.4 89.7 %shard_map.102 = (bf16[128,2048]{1,0:T(8,128)(2,1)}, bf16[128,2048]{1,0:T(8,128)(2,1)}, bf16[128,2048]{1,0:T(8,128)(2,1)}, f32[8,128]{1,0:T(8,128)}) custom-call(bf16[128,2048]{1,0:T(8,128)(2,1)} %bitcast.16, bf16[2,64,2048]{2,1,0:T(8,128)(2,1)} %bitcast.17, bf16[2,64,2048]{2,1,0:T(8,128)(2,1)} %bitcast.18, bf16[128,2048]{1,0:T(8,128)(2,1)} %bitcast.19, ...), custom_call_target="tpu_custom_call" | custom-call | flops 1342177280 | bytes 3670016 | tf_op jit(solution)/shard_map/pallas_call | solution.py:382
  93.1 1.2 %slice_bitcast_fusion = f32[16]{0:T(128)} fusion(f32[8,128]{1,0:T(8,128)} %get-tuple-element.11), kind=kLoop, calls=%fused_computation.48 | loop fusion | bytes 128 | tf_op jit(solution)/shard_map/squeeze | solution.py:434
  94.3 0.0 copy-start.2
  94.3 1.9 %copy.18 = bf16[128,1,2048]{2,0,1:T(8,128)(2,1)} copy(bf16[128,1,2048]{2,0,1:T(8,128)(2,1)} %bitcast.15) | data formatting | bytes 1048576
  96.2 0.0 copy-done.2
  96.2 0.0 copy-start.1
  96.2 0.8 copy.19
  97.0 0.4 copy-done.1
  97.5 0.8 copy.20
  (5 shorter events, 0.1 us)
Async XLA Ops:
  0.6 1.0 copy-start
  0.7 0.7 copy-start.3
  94.3 1.9 %copy-start.2 = (bf16[128,2048]{1,0:T(8,128)(2,1)S(1)}, bf16[128,2048]{1,0:T(8,128)(2,1)}, u32[]{:S(2)}) copy-start(bf16[128,2048]{1,0:T(8,128)(2,1)} %get-tuple-element.9) | copy-start | bytes 1572868
  96.2 1.2 %copy-start.1 = (bf16[128,2048]{1,0:T(8,128)(2,1)S(1)}, bf16[128,2048]{1,0:T(8,128)(2,1)}, u32[]{:S(2)}) copy-start(bf16[128,2048]{1,0:T(8,128)(2,1)} %get-tuple-element.10) | copy-start | bytes 1572868

commit v2 on v1

--- a/solution.py
+++ b/solution.py
@@ -86,7 +86,35 @@
         (g_in, gbuf, piece, 0),
         (v_in, vbuf, tok // span, 1),
     )
+
+    def prepare():
+        zero_block = jnp.zeros((span, width), BF16)
+        for buf in (kbuf, vbuf):
+            buf[0] = zero_block
+            buf[nblocks + 1] = zero_block
+
+        def clear(c, _):
+            dk_acc[c] = jnp.zeros((span, width), F32)
+            dv_acc[c] = jnp.zeros((span, width), F32)
+            return _
+
+        lax.fori_loop(0, nblocks + 2, clear, 0)
+        dk_anchor[...] = jnp.zeros_like(dk_anchor)
+        dv_anchor[...] = jnp.zeros_like(dv_anchor)
+        dk_chain[0] = jnp.zeros((span, width), F32)
+        dv_chain[0] = jnp.zeros((span, width), F32)
+        temp_acc[...] = jnp.zeros_like(temp_acc)
+
+    def sent(a):
+        _, target, rows, _ = arrivals[a]
+        ref = target.at[pl.ds(0, (n - 1) * rows)]
+        pltpu.make_async_copy(ref, ref, in_send.at[a]).wait()
+
     for a, (source, target, rows, shift) in enumerate(arrivals):
+        if a == 2:
+            prepare()
+        if a >= 2:
+            sent(a - 2)
 
         def block(d):
             if shift:
@@ -118,23 +146,6 @@
         ref = target.at[pl.ds(shift, n * rows)]
         pltpu.make_async_copy(ref, ref, in_recv.at[a]).wait()
 
-    zero_block = jnp.zeros((span, width), BF16)
-    for buf in (kbuf, vbuf):
-        buf[0] = zero_block
-        buf[nblocks + 1] = zero_block
-
-    def clear(c, _):
-        dk_acc[c] = jnp.zeros((span, width), F32)
-        dv_acc[c] = jnp.zeros((span, width), F32)
-        return _
-
-    lax.fori_loop(0, nblocks + 2, clear, 0)
-    dk_anchor[...] = jnp.zeros_like(dk_anchor)
-    dv_anchor[...] = jnp.zeros_like(dv_anchor)
-    dk_chain[0] = jnp.zeros((span, width), F32)
-    dv_chain[0] = jnp.zeros((span, width), F32)
-    temp_acc[...] = jnp.zeros_like(temp_acc)
-
     scale = scale_in[item % heads]
     alpha = scale * reciprocal
     anchors = [table[2 * entries + nblocks + x] for x in range(n_anchor)]
@@ -179,8 +190,12 @@
     arrive(0)
     arrive(1)
 
-    def scores(k, _):
-        for j in range(units):
+    group = 2 if units <= 2 else 1
+    steps = n // group
+    members = lambda i: [(i * group + y, j) for y in range(group) for j in range(units)]
+
+    def scores(i, _):
+        for k, j in members(i):
             at, blk, t = unit_at(k, j)
             s = lax.dot_general(
                 qbuf[at, :], select(kbuf, blk, t), rows_by_cols, preferred_element_type=F32
@@ -191,13 +206,13 @@
             p_ref[at, :] = e * (1.0 / jnp.sum(e, axis=1, keepdims=True))
         return _
 
-    lax.fori_loop(0, n, scores, 0)
+    lax.fori_loop(0, steps, scores, 0)
 
     arrive(2)
 
-    def value_terms(k, _):
+    def value_terms(i, _):
         got, places = [], []
-        for j in range(units):
+        for k, j in members(i):
             at, blk, t = unit_at(k, j)
             low = p_ref[at, :].astype(BF16)
             got.append(
@@ -207,7 +222,7 @@
         scatter(got, places, dv_acc, dv_anchor, dv_chain)
         return _
 
-    lax.fori_loop(0, n, value_terms, 0)
+    lax.fori_loop(0, steps, value_terms, 0)
 
     def send_back(source, rows, target, target_rows, x, k):
         d = (me + 1 + k) % n
@@ -254,9 +269,9 @@
 
     arrive(3)
 
-    def score_terms(k, _):
+    def score_terms(i, _):
         got, places = [], []
-        for j in range(units):
+        for k, j in members(i):
             at, blk, t = unit_at(k, j)
             dprob = lax.dot_general(
                 gbuf[at, :], select(vbuf, blk, t), rows_by_cols, preferred_element_type=F32
@@ -280,11 +295,12 @@
             )
             places.append((blk, t))
         mine_rows = pl.ds(pl.multiple_of(replica * piece, piece), piece)
-        send_back(dq_send, piece, q_out, mine_rows, 0, k)
+        for y in range(group):
+            send_back(dq_send, piece, q_out, mine_rows, 0, i * group + y)
         scatter(got, places, dk_acc, dk_anchor, dk_chain)
         return _
 
-    lax.fori_loop(0, n, score_terms, 0)
+    lax.fori_loop(0, steps, score_terms, 0)
     finish(dk_acc, dk_anchor, dk_chain, dk_send, k_out, 1)
 
     total = jnp.sum(temp_acc[...], axis=1, keepdims=True)
@@ -328,15 +344,45 @@
         result += jnp.where(lane == d // copies % heads, item_terms[d], 0.0)
     scale_out[...] = result
 
-    for a, (_, target, rows, _) in enumerate(arrivals):
-        ref = target.at[pl.ds(0, (n - 1) * rows)]
-        pltpu.make_async_copy(ref, ref, in_send.at[a]).wait()
+    sent(2)
+    sent(3)
     for x, (source, rows, target) in enumerate(
         ((dq_send, piece, q_out), (dk_send, tok, k_out), (dv_send, tok, v_out))
     ):
         ref = source.at[pl.ds(0, (n - 1) * rows)]
         pltpu.make_async_copy(ref, ref, out_send.at[x]).wait()
         pltpu.make_async_copy(target, target, out_recv.at[x]).wait()
+
+
+def hand_over(arrays, scales, heads):
+    count, chunks = len(arrays), 4
+
+    def kernel(*refs):
+        sources, scale_ref = refs[:count], refs[count]
+        targets, scale_out, sems = refs[count + 1 : -2], refs[-2], refs[-1]
+        copies = []
+        for x, (source, target) in enumerate(zip(sources, targets)):
+            rows = source.shape[0] // chunks
+            for y in range(chunks):
+                at = pl.ds(y * rows, rows)
+                copies.append(
+                    pltpu.make_async_copy(source.at[at], target.at[at], sems.at[x * chunks + y])
+                )
+                copies[-1].start()
+        scale_out[...] = scale_ref[0:1, :heads]
+        for copy in copies:
+            copy.wait()
+
+    anywhere = pl.BlockSpec(memory_space=pl.ANY)
+    local = pl.BlockSpec(memory_space=pltpu.VMEM)
+    return pl.pallas_call(
+        kernel,
+        out_shape=[jax.ShapeDtypeStruct(a.shape, a.dtype) for a in arrays]
+        + [jax.ShapeDtypeStruct((1, heads), F32)],
+        in_specs=[anywhere] * count + [local],
+        out_specs=[anywhere] * count + [local],
+        scratch_shapes=[pltpu.SemaphoreType.DMA((count * chunks,))],
+    )(*arrays, scales)
 
 
 def slot_table(anchor_tiles, sampled_tiles, head, blocks, nblocks):
@@ -426,12 +472,16 @@
     )(flat(probe), tiled(matcher), tiled(payload), flat(adjoint), logit_scale, table)
 
     def combine(received):
-        if copies > 1:
-            pieces = received.astype(F32).reshape(tok, heads, copies, width)
-            received = jnp.sum(pieces, axis=2).astype(BF16)
-        return received.reshape(tok, seq_count, total_width)
-
-    return q_out.reshape(probe.shape), combine(k_out), combine(v_out), scales[0, :heads]
+        pieces = received.astype(F32).reshape(tok, heads, copies, width)
+        return jnp.sum(pieces, axis=2).astype(BF16)
+
+    if copies == 1:
+        q_out, k_out, v_out, scales = hand_over((q_out, k_out, v_out), scales, heads)
+    else:
+        q_out, scales = hand_over((q_out,), scales, heads)
+        k_out, v_out = combine(k_out), combine(v_out)
+    shaped = lambda array: array.reshape(probe.shape)
+    return shaped(q_out), shaped(k_out), shaped(v_out), scales.reshape(heads)
 
 
 def solution(mesh):

time: 98.6 us -> 143 us (1.45)
  Pallas kernels: 89.7 us -> 140 us
  local copies, waits for them, and re-layouts: 6.78 us -> 1.63 us
    pallas_call x0 -> x1, Pallas kernels: none -> 50 us  [hand_over(): pl.pallas_call(kernel, out_shape=[jax.ShapeDtypeStruct(a.shape, a.dtype)...]
    unnamed x11 -> x4, local copies, waits for them, and re-layouts: 4.64 us -> 0.67 us
where the time goes in v2:
time: 143 us
  Pallas kernels  140 us (98%)
  local copies, waits for them, and re-layouts  1.63 us (1%)
    pallas_call x1, Pallas kernels, on_device(): pl.pallas_call(functools.partial(attention_kernel, dims), out_shape=(jax....  89.7 us
    pallas_call x1, Pallas kernels, hand_over(): pl.pallas_call(kernel, out_shape=[jax.ShapeDtypeStruct(a.shape, a.dtype)...  50 us

profile of v2, /device:TPU:0, one launch (start us, length us, event | category | flops | bytes accessed | tf_op | source)
XLA Modules:
  0.0 143.1 jit_solution(6785656836135804479)
XLA Ops:
  0.6 0.0 copy-start
  0.7 0.0 copy-start.1
  0.7 0.7 copy-done.1
  1.3 0.2 dynamic-slice_reduce_fusion
  1.6 0.0 copy-done
  1.6 0.1 copy.14
  1.7 0.6 gather_fusion
  2.3 0.1 broadcast_select_fusion
  2.4 0.1 select_n.131
  2.5 0.1 select_reduce_fusion.1
  2.6 0.2 select_reduce_fusion
  2.8 0.6 pad_add_fusion.table
  3.4 89.7 %shard_map.102 = (bf16[128,2048]{1,0:T(8,128)(2,1)}, bf16[128,2048]{1,0:T(8,128)(2,1)}, bf16[128,2048]{1,0:T(8,128)(2,1)}, f32[8,128]{1,0:T(8,128)}) custom-call(bf16[128,2048]{1,0:T(8,128)(2,1)} %bitcast.12, bf16[2,64,2048]{2,1,0:T(8,128)(2,1)} %bitcast.13, bf16[2,64,2048]{2,1,0:T(8,128)(2,1)} %bitcast.14, bf16[128,2048]{1,0:T(8,128)(2,1)} %bitcast.15, ...), custom_call_target="tpu_custom_call" | custom-call | flops 1342177280 | bytes 3670016 | tf_op jit(solution)/shard_map/pallas_call | solution.py:428
  93.1 50.0 %shard_map.103 = (bf16[128,2048]{1,0:T(8,128)(2,1)}, bf16[128,2048]{1,0:T(8,128)(2,1)}, bf16[128,2048]{1,0:T(8,128)(2,1)}, f32[1,16]{1,0:T(1,128)}) custom-call(bf16[128,2048]{1,0:T(8,128)(2,1)} %get-tuple-element.12.refs_0_, bf16[128,2048]{1,0:T(8,128)(2,1)} %get-tuple-element.13.refs_1_, bf16[128,2048]{1,0:T(8,128)(2,1)} %get-tuple-element.14.refs_2_, ...), custom_call_target="tpu_custom_call" | custom-call | tf_op jit(solution)/shard_map/pallas_call | solution.py:378
  (5 shorter events, 0.1 us)
Async XLA Ops:
  0.6 1.0 copy-start
  0.7 0.7 copy-start.1

commit v3 on v2

--- a/solution.py
+++ b/solution.py
@@ -9,10 +9,16 @@
 from jax.sharding import PartitionSpec as P
 
 TILE_SPAN = 64
+STRIDE = 5
 MASKED = -1e30
 MESH = pl.DeviceIdType.MESH
 F32 = jnp.float32
 BF16 = jnp.bfloat16
+
+
+def peer_of(me, i, n):
+    stride = STRIDE if math.gcd(STRIDE, n) == 1 else 1
+    return (me + i * stride) % n
 
 
 def attention_kernel(
@@ -127,7 +133,7 @@
             landing = target.at[pl.ds(pl.multiple_of(me * rows, rows), rows)]
 
         def send(o, _):
-            d = (me + o) % n
+            d = peer_of(me, o, n)
             pltpu.make_async_remote_copy(
                 src_ref=block(d),
                 dst_ref=landing,
@@ -153,7 +159,7 @@
     slot_of = lax.broadcasted_iota(jnp.int32, (1, slots * span), 1) // span
 
     def unit_at(k, j):
-        p = (me + 1 + k) % n
+        p = peer_of(me, k + 1, n)
         row = pl.multiple_of(p * piece + j * tile, tile)
         blk = (p * tok + replica * piece + j * tile) // span
         return pl.ds(row, tile), blk, k * units + j
@@ -225,7 +231,7 @@
     lax.fori_loop(0, steps, value_terms, 0)
 
     def send_back(source, rows, target, target_rows, x, k):
-        d = (me + 1 + k) % n
+        d = peer_of(me, k + 1, n)
         block = source.at[pl.ds(pl.multiple_of(d * rows, rows), rows)]
 
         @pl.when(k < n - 1)
@@ -252,7 +258,7 @@
 
     def finish(acc, anchor, chain, source, target, x):
         def step(k, _):
-            d = (me + 1 + k) % n
+            d = peer_of(me, k + 1, n)
             for b in range(tok // span):
                 c = d * (tok // span) + b
                 last = table[2 * entries + c]
@@ -355,20 +361,15 @@
 
 
 def hand_over(arrays, scales, heads):
-    count, chunks = len(arrays), 4
+    count = len(arrays)
 
     def kernel(*refs):
         sources, scale_ref = refs[:count], refs[count]
         targets, scale_out, sems = refs[count + 1 : -2], refs[-2], refs[-1]
         copies = []
         for x, (source, target) in enumerate(zip(sources, targets)):
-            rows = source.shape[0] // chunks
-            for y in range(chunks):
-                at = pl.ds(y * rows, rows)
-                copies.append(
-                    pltpu.make_async_copy(source.at[at], target.at[at], sems.at[x * chunks + y])
-                )
-                copies[-1].start()
+            copies.append(pltpu.make_async_copy(source, target, sems.at[x]))
+            copies[-1].start()
         scale_out[...] = scale_ref[0:1, :heads]
         for copy in copies:
             copy.wait()
@@ -379,9 +380,9 @@
         kernel,
         out_shape=[jax.ShapeDtypeStruct(a.shape, a.dtype) for a in arrays]
         + [jax.ShapeDtypeStruct((1, heads), F32)],
-        in_specs=[anywhere] * count + [local],
+        in_specs=[local] * count + [local],
         out_specs=[anywhere] * count + [local],
-        scratch_shapes=[pltpu.SemaphoreType.DMA((count * chunks,))],
+        scratch_shapes=[pltpu.SemaphoreType.DMA((count,))],
     )(*arrays, scales)
 
 
@@ -410,7 +411,7 @@
     nblocks = n * tok // TILE_SPAN
     me = lax.axis_index("seq")
     order = jnp.arange(n * units, dtype=jnp.int32)
-    peer = (me + 1 + order // units) % n
+    peer = peer_of(me, order // units + 1, n)
     blocks = (peer * tok + me % copies * piece + order % units * tile) // TILE_SPAN
     table = slot_table(anchor_tiles, sampled_tiles, me // copies % heads, blocks, nblocks)
 

time: 143 us -> 96.2 us (0.67)
  Pallas kernels: 140 us -> 92.6 us
    pallas_call x1, Pallas kernels: 50 us -> 3.03 us  [hand_over(): pl.pallas_call(kernel, out_shape=[jax.ShapeDtypeStruct(a.shape, a.dtype)...]
where the time goes in v3:
time: 96.2 us; the launch traced here: 96 us
  Pallas kernels  92.6 us (96%)
  local copies, waits for them, and re-layouts  1.63 us (2%)
  other arithmetic  1.09 us (1%)
    pallas_call x1, Pallas kernels, on_device(): pl.pallas_call(functools.partial(attention_kernel, dims), out_shape=(jax....  89.6 us
    pallas_call x1, Pallas kernels, hand_over(): pl.pallas_call(kernel, out_shape=[jax.ShapeDtypeStruct(a.shape, a.dtype)...  3.03 us

profile of v3, /device:TPU:0, one launch (start us, length us, event | category | flops | bytes accessed | tf_op | source)
XLA Modules:
  0.0 96.0 jit_solution(13382902108821979155)
XLA Ops:
  0.6 0.0 copy-start
  0.7 0.0 copy-start.1
  0.7 0.7 copy-done.1
  1.3 0.2 dynamic-slice_reduce_fusion
  1.6 0.0 copy-done
  1.6 0.1 copy.14
  1.7 0.6 gather_fusion
  2.3 0.1 broadcast_select_fusion
  2.4 0.1 select_n.131
  2.5 0.1 select_reduce_fusion.1
  2.6 0.2 select_reduce_fusion
  2.8 0.6 pad_add_fusion.table
  3.4 89.6 %shard_map.102 = (bf16[128,2048]{1,0:T(8,128)(2,1)}, bf16[128,2048]{1,0:T(8,128)(2,1)}, bf16[128,2048]{1,0:T(8,128)(2,1)}, f32[8,128]{1,0:T(8,128)}) custom-call(bf16[128,2048]{1,0:T(8,128)(2,1)} %bitcast.12, bf16[2,64,2048]{2,1,0:T(8,128)(2,1)} %bitcast.13, bf16[2,64,2048]{2,1,0:T(8,128)(2,1)} %bitcast.14, bf16[128,2048]{1,0:T(8,128)(2,1)} %bitcast.15, ...), custom_call_target="tpu_custom_call" | custom-call | flops 1342177280 | bytes 3670016 | tf_op jit(solution)/shard_map/pallas_call | solution.py:429
  93.0 3.0 %shard_map.103 = (bf16[128,2048]{1,0:T(8,128)(2,1)}, bf16[128,2048]{1,0:T(8,128)(2,1)}, bf16[128,2048]{1,0:T(8,128)(2,1)}, f32[1,16]{1,0:T(1,128)}) custom-call(bf16[128,2048]{1,0:T(8,128)(2,1)} %get-tuple-element.12.refs_0_, bf16[128,2048]{1,0:T(8,128)(2,1)} %get-tuple-element.13.refs_1_, bf16[128,2048]{1,0:T(8,128)(2,1)} %get-tuple-element.14.refs_2_, ...), custom_call_target="tpu_custom_call" | custom-call | tf_op jit(solution)/shard_map/pallas_call | solution.py:379
  (5 shorter events, 0.1 us)
Async XLA Ops:
  0.6 1.0 copy-start
  0.7 0.7 copy-start.1

commit v4 on v3

--- a/solution.py
+++ b/solution.py
@@ -16,9 +16,16 @@
 BF16 = jnp.bfloat16
 
 
+def stride_of(n):
+    return STRIDE if math.gcd(STRIDE, n) == 1 else 1
+
+
 def peer_of(me, i, n):
-    stride = STRIDE if math.gcd(STRIDE, n) == 1 else 1
-    return (me + i * stride) % n
+    return (me + i * stride_of(n)) % n
+
+
+def turn_of(me, peer, n):
+    return ((peer - me + n) * pow(stride_of(n), -1, n) + n - 1) % n
 
 
 def attention_kernel(
@@ -162,14 +169,14 @@
         p = peer_of(me, k + 1, n)
         row = pl.multiple_of(p * piece + j * tile, tile)
         blk = (p * tok + replica * piece + j * tile) // span
-        return pl.ds(row, tile), blk, k * units + j
+        return pl.ds(row, tile), blk, (k * units + j, p * units + j)
 
     def select(buf, blk, t):
         parts = [buf[pl.ds(blk, 3)].reshape(window, width)]
         for a in anchors:
             parts.append(buf[a + 1])
         for x in range(n_random):
-            parts.append(buf[table[t * n_random + x] + 1])
+            parts.append(buf[table[t[1] * n_random + x] + 1])
         return jnp.concatenate(parts, axis=0)
 
     def bias_of(blk):
@@ -180,15 +187,15 @@
             bias = jnp.where(slot_of == 3 + x, off(jnp.abs(a - blk) <= 1), bias)
         return bias
 
-    def scatter(got, places, acc, anchor, chain):
+    def scatter(d, blk, t, acc, anchor, chain):
         base = window + n_anchor * span
-        for (blk, t), d in zip(places, got):
-            acc[pl.ds(blk, 3)] += d[:window].reshape(3, span, width)
-            anchor[...] += d[window:base].reshape(n_anchor, span, width)
-            for x in range(n_random):
-                e = t * n_random + x
-                before = table[entries + e]
-                chain[e + 1] = chain[before] + d[base + x * span : base + (x + 1) * span]
+        acc[pl.ds(blk, 3)] += d[:window].reshape(3, span, width)
+        anchor[...] += d[window:base].reshape(n_anchor, span, width)
+        for x in range(n_random):
+            before = table[entries + t[1] * n_random + x]
+            chain[t[0] * n_random + x + 1] = (
+                chain[before] + d[base + x * span : base + (x + 1) * span]
+            )
 
     rows_by_cols = (((1,), (1,)), ((), ()))
     over_rows = (((0,), (0,)), ((), ()))
@@ -217,15 +224,11 @@
     arrive(2)
 
     def value_terms(i, _):
-        got, places = [], []
         for k, j in members(i):
             at, blk, t = unit_at(k, j)
             low = p_ref[at, :].astype(BF16)
-            got.append(
-                lax.dot_general(low, gbuf[at, :], over_rows, preferred_element_type=F32)
-            )
-            places.append((blk, t))
-        scatter(got, places, dv_acc, dv_anchor, dv_chain)
+            dv = lax.dot_general(low, gbuf[at, :], over_rows, preferred_element_type=F32)
+            scatter(dv, blk, t, dv_acc, dv_anchor, dv_chain)
         return _
 
     lax.fori_loop(0, steps, value_terms, 0)
@@ -276,7 +279,6 @@
     arrive(3)
 
     def score_terms(i, _):
-        got, places = [], []
         for k, j in members(i):
             at, blk, t = unit_at(k, j)
             dprob = lax.dot_general(
@@ -296,14 +298,11 @@
             draw = (dscore * alpha).astype(BF16)
             dq = jnp.dot(draw, select(kbuf, blk, t), preferred_element_type=F32)
             dq_send[at, :] = dq.astype(BF16)
-            got.append(
-                lax.dot_general(draw, qbuf[at, :], over_rows, preferred_element_type=F32)
-            )
-            places.append((blk, t))
+            dk = lax.dot_general(draw, qbuf[at, :], over_rows, preferred_element_type=F32)
+            scatter(dk, blk, t, dk_acc, dk_anchor, dk_chain)
         mine_rows = pl.ds(pl.multiple_of(replica * piece, piece), piece)
         for y in range(group):
             send_back(dq_send, piece, q_out, mine_rows, 0, i * group + y)
-        scatter(got, places, dk_acc, dk_anchor, dk_chain)
         return _
 
     lax.fori_loop(0, steps, score_terms, 0)
@@ -361,17 +360,30 @@
 
 
 def hand_over(arrays, scales, heads):
-    count = len(arrays)
+    count, halves = len(arrays), 2
+    tok, total_width = arrays[0].shape
+    rows = tok // halves
 
     def kernel(*refs):
         sources, scale_ref = refs[:count], refs[count]
-        targets, scale_out, sems = refs[count + 1 : -2], refs[-2], refs[-1]
-        copies = []
-        for x, (source, target) in enumerate(zip(sources, targets)):
-            copies.append(pltpu.make_async_copy(source, target, sems.at[x]))
-            copies[-1].start()
+        targets, scale_out = refs[count + 1 : -4], refs[-4]
+        held, arrived, left = refs[-3:]
+        pieces = [(x, y, pl.ds(y * rows, rows)) for x in range(count) for y in range(halves)]
+        ins = [
+            pltpu.make_async_copy(sources[x].at[at], held.at[x, at], arrived.at[x, y])
+            for x, y, at in pieces
+        ]
+        outs = [
+            pltpu.make_async_copy(held.at[x, at], targets[x].at[at], left.at[x, y])
+            for x, y, at in pieces
+        ]
+        for copy in ins:
+            copy.start()
         scale_out[...] = scale_ref[0:1, :heads]
-        for copy in copies:
+        for first, second in zip(ins, outs):
+            first.wait()
+            second.start()
+        for copy in outs:
             copy.wait()
 
     anywhere = pl.BlockSpec(memory_space=pl.ANY)
@@ -380,22 +392,25 @@
         kernel,
         out_shape=[jax.ShapeDtypeStruct(a.shape, a.dtype) for a in arrays]
         + [jax.ShapeDtypeStruct((1, heads), F32)],
-        in_specs=[local] * count + [local],
+        in_specs=[anywhere] * count + [local],
         out_specs=[anywhere] * count + [local],
-        scratch_shapes=[pltpu.SemaphoreType.DMA((count,))],
+        scratch_shapes=[
+            pltpu.VMEM((count, tok, total_width), BF16),
+            pltpu.SemaphoreType.DMA((count, halves)),
+            pltpu.SemaphoreType.DMA((count, halves)),
+        ],
     )(*arrays, scales)
 
 
-def slot_table(anchor_tiles, sampled_tiles, head, blocks, nblocks):
-    tiles = jnp.take(lax.dynamic_index_in_dim(sampled_tiles, head, 0, False), blocks, axis=0)
-    tiles = tiles.reshape(-1).astype(jnp.int32)
-    place = jnp.arange(tiles.shape[0], dtype=jnp.int32)
+def slot_table(anchors, tiles, order, nblocks):
+    tiles = tiles.astype(jnp.int32)
+    place = order[:, None] * tiles.shape[1] + jnp.arange(tiles.shape[1], dtype=jnp.int32)
+    tiles, place = tiles.reshape(-1), place.reshape(-1)
     earlier = (tiles[:, None] == tiles[None, :]) & (place[None, :] < place[:, None])
     before = jnp.max(jnp.where(earlier, place[None, :] + 1, 0), axis=1)
     ids = jnp.arange(nblocks, dtype=jnp.int32)
     last = jnp.max(jnp.where(tiles[None, :] == ids[:, None], place[None, :] + 1, 0), axis=1)
-    anchors = lax.dynamic_index_in_dim(anchor_tiles, head, 0, False).astype(jnp.int32)
-    return jnp.concatenate([tiles, before, last, anchors])
+    return jnp.concatenate([tiles, before, last, anchors.astype(jnp.int32)])
 
 
 def on_device(n, nf, probe, matcher, payload, adjoint, logit_scale, anchor_tiles, sampled_tiles):
@@ -410,10 +425,15 @@
     n_anchor, n_random = anchor_tiles.shape[1], sampled_tiles.shape[2]
     nblocks = n * tok // TILE_SPAN
     me = lax.axis_index("seq")
-    order = jnp.arange(n * units, dtype=jnp.int32)
-    peer = peer_of(me, order // units + 1, n)
-    blocks = (peer * tok + me % copies * piece + order % units * tile) // TILE_SPAN
-    table = slot_table(anchor_tiles, sampled_tiles, me // copies % heads, blocks, nblocks)
+    head = me // copies % heads
+    unit = jnp.arange(n * units, dtype=jnp.int32)
+    order = turn_of(me, unit // units, n) * units + unit % units
+    tiles = lax.dynamic_index_in_dim(sampled_tiles, head, 0, False)
+    anchors = lax.dynamic_index_in_dim(anchor_tiles, head, 0, False)
+    if copies > 1:
+        blocks = (unit // units * tok + me % copies * piece + unit % units * tile) // TILE_SPAN
+        tiles = jnp.take(tiles, blocks, axis=0)
+    table = slot_table(anchors, tiles, order, nblocks)
 
     dims = (n, nf, copies, tok, piece, tile, width, heads, n_anchor, n_random)
     keys = n * tok

time: 96.2 us -> 96.1 us (level)
  no operation moved by 1% of the time
where the time goes in v4:
time: 96.1 us; the launch traced here: 95.8 us
  Pallas kernels  92.9 us (97%)
  local copies, waits for them, and re-layouts  1.18 us (1%)
  other arithmetic  1.04 us (1%)
    pallas_call x1, Pallas kernels, on_device(): pl.pallas_call(functools.partial(attention_kernel, dims), out_shape=(jax....  89.6 us
    pallas_call x1, Pallas kernels, hand_over(): pl.pallas_call(kernel, out_shape=[jax.ShapeDtypeStruct(a.shape, a.dtype)...  3.37 us

profile of v4, /device:TPU:0, one launch (start us, length us, event | category | flops | bytes accessed | tf_op | source)
XLA Modules:
  0.0 95.8 jit_solution(16658549007532544285)
XLA Ops:
  0.6 0.0 copy-start
  0.7 0.0 copy-start.1
  0.7 0.7 copy-done.1
  1.4 0.2 dynamic-slice_reduce_fusion
  1.5 0.0 copy-done
  1.6 0.1 copy.13
  1.7 0.1 reshape.121
  1.8 0.1 iota_add_fusion
  1.8 0.1 add.103
  2.0 0.2 select_reduce_fusion
  2.1 0.1 select_reduce_fusion.1
  2.3 0.6 pad_add_fusion.table
  2.9 89.6 %shard_map.102 = (bf16[128,2048]{1,0:T(8,128)(2,1)}, bf16[128,2048]{1,0:T(8,128)(2,1)}, bf16[128,2048]{1,0:T(8,128)(2,1)}, f32[8,128]{1,0:T(8,128)}) custom-call(bf16[128,2048]{1,0:T(8,128)(2,1)} %bitcast.8, bf16[2,64,2048]{2,1,0:T(8,128)(2,1)} %bitcast.9, bf16[2,64,2048]{2,1,0:T(8,128)(2,1)} %bitcast.10, bf16[128,2048]{1,0:T(8,128)(2,1)} %bitcast.11, ...), custom_call_target="tpu_custom_call" | custom-call | flops 1342177280 | bytes 3670016 | tf_op jit(solution)/shard_map/pallas_call | solution.py:449
  92.5 3.4 %shard_map.103 = (bf16[128,2048]{1,0:T(8,128)(2,1)}, bf16[128,2048]{1,0:T(8,128)(2,1)}, bf16[128,2048]{1,0:T(8,128)(2,1)}, f32[1,16]{1,0:T(1,128)}) custom-call(bf16[128,2048]{1,0:T(8,128)(2,1)} %get-tuple-element.12.refs_0_, bf16[128,2048]{1,0:T(8,128)(2,1)} %get-tuple-element.13.refs_1_, bf16[128,2048]{1,0:T(8,128)(2,1)} %get-tuple-element.14.refs_2_, ...), custom_call_target="tpu_custom_call" | custom-call | tf_op jit(solution)/shard_map/pallas_call | solution.py:391
  (3 shorter events, 0.0 us)
Async XLA Ops:
  0.6 0.9 copy-start
  0.7 0.7 copy-start.1

commit v5 on v4

--- a/solution.py
+++ b/solution.py
@@ -360,30 +360,17 @@
 
 
 def hand_over(arrays, scales, heads):
-    count, halves = len(arrays), 2
-    tok, total_width = arrays[0].shape
-    rows = tok // halves
+    count = len(arrays)
 
     def kernel(*refs):
         sources, scale_ref = refs[:count], refs[count]
-        targets, scale_out = refs[count + 1 : -4], refs[-4]
-        held, arrived, left = refs[-3:]
-        pieces = [(x, y, pl.ds(y * rows, rows)) for x in range(count) for y in range(halves)]
-        ins = [
-            pltpu.make_async_copy(sources[x].at[at], held.at[x, at], arrived.at[x, y])
-            for x, y, at in pieces
-        ]
-        outs = [
-            pltpu.make_async_copy(held.at[x, at], targets[x].at[at], left.at[x, y])
-            for x, y, at in pieces
-        ]
-        for copy in ins:
-            copy.start()
+        targets, scale_out, sems = refs[count + 1 : -2], refs[-2], refs[-1]
+        copies = []
+        for x, (source, target) in enumerate(zip(sources, targets)):
+            copies.append(pltpu.make_async_copy(source, target, sems.at[x]))
+            copies[-1].start()
         scale_out[...] = scale_ref[0:1, :heads]
-        for first, second in zip(ins, outs):
-            first.wait()
-            second.start()
-        for copy in outs:
+        for copy in copies:
             copy.wait()
 
     anywhere = pl.BlockSpec(memory_space=pl.ANY)
@@ -392,13 +379,9 @@
         kernel,
         out_shape=[jax.ShapeDtypeStruct(a.shape, a.dtype) for a in arrays]
         + [jax.ShapeDtypeStruct((1, heads), F32)],
-        in_specs=[anywhere] * count + [local],
+        in_specs=[local] * count + [local],
         out_specs=[anywhere] * count + [local],
-        scratch_shapes=[
-            pltpu.VMEM((count, tok, total_width), BF16),
-            pltpu.SemaphoreType.DMA((count, halves)),
-            pltpu.SemaphoreType.DMA((count, halves)),
-        ],
+        scratch_shapes=[pltpu.SemaphoreType.DMA((count,))],
     )(*arrays, scales)
 
 
@@ -441,6 +424,9 @@
     slots = (3 + n_anchor + n_random) * TILE_SPAN
     chain = (n * units * n_random + 1, TILE_SPAN, width)
     padded = (nblocks + 2, TILE_SPAN, width)
+    kept = 2 * (3 * queries + 2 * keys + 2 * nblocks * TILE_SPAN) * width
+    kept += 4 * (2 * queries * slots + 2 * math.prod(padded) + 2 * math.prod(chain))
+    needed = kept + 10 * 1024 * 1024
     anywhere = pl.BlockSpec(memory_space=pl.ANY)
     scalars = pl.BlockSpec(memory_space=pltpu.SMEM)
     flat = lambda array: array.reshape(tok, total_width)
@@ -454,7 +440,7 @@
             parts,
             jax.ShapeDtypeStruct((8, 128), F32),
         ),
-        in_specs=[anywhere] * 4 + [scalars] * 2,
+        in_specs=[pl.BlockSpec(memory_space=pltpu.HBM)] * 4 + [scalars] * 2,
         out_specs=(anywhere, anywhere, anywhere, pl.BlockSpec(memory_space=pltpu.VMEM)),
         scratch_shapes=[
             pltpu.VMEM((queries, width), BF16),
@@ -483,7 +469,7 @@
             pltpu.SemaphoreType.DMA((2,)),
         ],
         compiler_params=pltpu.CompilerParams(
-            collective_id=0, has_side_effects=True, vmem_limit_bytes=56 * 1024 * 1024
+            collective_id=0, has_side_effects=True, vmem_limit_bytes=needed
         ),
         cost_estimate=pl.CostEstimate(
             flops=10 * queries * slots * width,

time: 96.1 us -> 102 us (1.061)
  local copies, waits for them, and re-layouts: 1.18 us -> 8.9 us
  Pallas kernels: 92.9 us -> 91.6 us
    unnamed x4 -> x22, local copies, waits for them, and re-layouts: 0.68 us -> 8.41 us
where the time goes in v5:
time: 102 us
  Pallas kernels  91.6 us (90%)
  local copies, waits for them, and re-layouts  8.9 us (9%)
    pallas_call x1, Pallas kernels, on_device(): pl.pallas_call(functools.partial(attention_kernel, dims), out_shape=(jax....  88.6 us
    unnamed x22, local copies, waits for them, and re-layouts  8.41 us
    pallas_call x1, Pallas kernels, hand_over(): pl.pallas_call(kernel, out_shape=[jax.ShapeDtypeStruct(a.shape, a.dtype)...  3.03 us

profile of v5, /device:TPU:0, one launch (start us, length us, event | category | flops | bytes accessed | tf_op | source)
XLA Modules:
  0.0 101.7 jit_solution(6207110347877770411)
XLA Ops:
  0.6 0.0 copy-start
  0.7 0.0 copy-start.10
  0.7 0.7 copy-done.10
  1.4 0.2 dynamic-slice_reduce_fusion
  1.5 0.0 copy-done
  1.6 0.1 copy.13
  1.7 0.1 reshape.121
  1.8 0.1 iota_add_fusion
  1.8 0.1 add.103
  2.0 0.2 select_reduce_fusion
  2.1 0.1 select_reduce_fusion.1
  2.3 0.0 copy-start.9
  2.3 0.1 pad_add_fusion.table
  2.4 0.6 copy-done.9
  2.9 0.0 copy-start.5
  2.9 1.0 %copy-done.5 = bf16[128,1,2048]{2,0,1:T(8,128)(2,1)S(1)} copy-done((bf16[128,1,2048]{2,0,1:T(8,128)(2,1)S(1)}, bf16[128,1,2048]{2,0,1:T(8,128)(2,1)}, u32[]{:S(2)}) %copy-start.5) | copy-done | bytes 524312
  4.0 0.0 copy-start.6
  4.0 1.0 %copy-done.6 = bf16[128,1,2048]{2,0,1:T(8,128)(2,1)S(1)} copy-done((bf16[128,1,2048]{2,0,1:T(8,128)(2,1)S(1)}, bf16[128,1,2048]{2,0,1:T(8,128)(2,1)}, u32[]{:S(2)}) %copy-start.6) | copy-done | bytes 524312
  5.0 0.0 copy-start.7
  5.0 1.0 %copy-done.7 = bf16[128,1,2048]{2,0,1:T(8,128)(2,1)S(1)} copy-done((bf16[128,1,2048]{2,0,1:T(8,128)(2,1)S(1)}, bf16[128,1,2048]{2,0,1:T(8,128)(2,1)}, u32[]{:S(2)}) %copy-start.7) | copy-done | bytes 524312
  6.0 0.0 copy-start.8
  6.1 1.0 %copy-done.8 = bf16[128,1,2048]{2,0,1:T(8,128)(2,1)S(1)} copy-done((bf16[128,1,2048]{2,0,1:T(8,128)(2,1)S(1)}, bf16[128,1,2048]{2,0,1:T(8,128)(2,1)}, u32[]{:S(2)}) %copy-start.8) | copy-done | bytes 524312
  7.1 88.6 %shard_map.102 = (bf16[128,2048]{1,0:T(8,128)(2,1)S(1)}, bf16[128,2048]{1,0:T(8,128)(2,1)S(1)}, bf16[128,2048]{1,0:T(8,128)(2,1)S(1)}, f32[8,128]{1,0:T(8,128)S(1)}) custom-call(bf16[128,2048]{1,0:T(8,128)(2,1)S(1)} %bitcast.8, bf16[2,64,2048]{2,1,0:T(8,128)(2,1)S(1)} %bitcast.9, bf16[2,64,2048]{2,1,0:T(8,128)(2,1)S(1)} %bitcast.10, ...), custom_call_target="tpu_custom_call" | custom-call | flops 1342177280 | bytes 3670016 | tf_op jit(solution)/shard_map/pallas_call | solution.py:435
  95.7 0.0 copy-start.1
  95.7 0.8 copy-done.1
  96.5 0.0 copy-start.2
  96.5 0.8 copy-done.2
  97.3 0.0 copy-start.3
  97.3 0.8 copy-done.3
  98.1 0.0 copy-start.4
  98.1 0.6 copy-done.4
  98.7 3.0 %shard_map.103 = (bf16[128,2048]{1,0:T(8,128)(2,1)}, bf16[128,2048]{1,0:T(8,128)(2,1)}, bf16[128,2048]{1,0:T(8,128)(2,1)}, f32[1,16]{1,0:T(1,128)}) custom-call(bf16[128,2048]{1,0:T(8,128)(2,1)} %copy-done.1, bf16[128,2048]{1,0:T(8,128)(2,1)} %copy-done.2, bf16[128,2048]{1,0:T(8,128)(2,1)} %copy-done.3, f32[8,128]{1,0:T(8,128)} %copy-done.4), custom_call_target="tpu_custom_call" | custom-call | tf_op jit(solution)/shard_map/pallas_call | solution.py:378
  (3 shorter events, 0.0 us)
Async XLA Ops:
  0.6 0.9 copy-start
  0.7 0.7 copy-start.10
  2.3 0.7 copy-start.9
  2.9 1.0 %copy-start.5 = (bf16[128,1,2048]{2,0,1:T(8,128)(2,1)S(1)}, bf16[128,1,2048]{2,0,1:T(8,128)(2,1)}, u32[]{:S(2)}) copy-start(bf16[128,1,2048]{2,0,1:T(8,128)(2,1)} %param.7) | copy-start | bytes 1572868
  4.0 1.0 %copy-start.6 = (bf16[128,1,2048]{2,0,1:T(8,128)(2,1)S(1)}, bf16[128,1,2048]{2,0,1:T(8,128)(2,1)}, u32[]{:S(2)}) copy-start(bf16[128,1,2048]{2,0,1:T(8,128)(2,1)} %param.8) | copy-start | bytes 1572868
  5.0 1.0 %copy-start.7 = (bf16[128,1,2048]{2,0,1:T(8,128)(2,1)S(1)}, bf16[128,1,2048]{2,0,1:T(8,128)(2,1)}, u32[]{:S(2)}) copy-start(bf16[128,1,2048]{2,0,1:T(8,128)(2,1)} %param.9) | copy-start | bytes 1572868
  6.0 1.0 %copy-start.8 = (bf16[128,1,2048]{2,0,1:T(8,128)(2,1)S(1)}, bf16[128,1,2048]{2,0,1:T(8,128)(2,1)}, u32[]{:S(2)}) copy-start(bf16[128,1,2048]{2,0,1:T(8,128)(2,1)} %param.10) | copy-start | bytes 1572868
  95.7 0.8 copy-start.1
  96.5 0.8 copy-start.2
  97.3 0.8 copy-start.3
  98.1 0.6 copy-start.4

commit v6 on v5

--- a/solution.py
+++ b/solution.py
@@ -424,9 +424,6 @@
     slots = (3 + n_anchor + n_random) * TILE_SPAN
     chain = (n * units * n_random + 1, TILE_SPAN, width)
     padded = (nblocks + 2, TILE_SPAN, width)
-    kept = 2 * (3 * queries + 2 * keys + 2 * nblocks * TILE_SPAN) * width
-    kept += 4 * (2 * queries * slots + 2 * math.prod(padded) + 2 * math.prod(chain))
-    needed = kept + 10 * 1024 * 1024
     anywhere = pl.BlockSpec(memory_space=pl.ANY)
     scalars = pl.BlockSpec(memory_space=pltpu.SMEM)
     flat = lambda array: array.reshape(tok, total_width)
@@ -440,7 +437,7 @@
             parts,
             jax.ShapeDtypeStruct((8, 128), F32),
         ),
-        in_specs=[pl.BlockSpec(memory_space=pltpu.HBM)] * 4 + [scalars] * 2,
+        in_specs=[anywhere] * 4 + [scalars] * 2,
         out_specs=(anywhere, anywhere, anywhere, pl.BlockSpec(memory_space=pltpu.VMEM)),
         scratch_shapes=[
             pltpu.VMEM((queries, width), BF16),
@@ -469,7 +466,7 @@
             pltpu.SemaphoreType.DMA((2,)),
         ],
         compiler_params=pltpu.CompilerParams(
-            collective_id=0, has_side_effects=True, vmem_limit_bytes=needed
+            collective_id=0, has_side_effects=True, vmem_limit_bytes=56 * 1024 * 1024
         ),
         cost_estimate=pl.CostEstimate(
             flops=10 * queries * slots * width,

time: 102 us -> 95.7 us (0.938)
  local copies, waits for them, and re-layouts: 8.9 us -> 1.18 us
    unnamed x22 -> x4, local copies, waits for them, and re-layouts: 8.41 us -> 0.68 us
where the time goes in v6:
time: 95.7 us; the launch traced here: 95.5 us
  Pallas kernels  92.6 us (97%)
  local copies, waits for them, and re-layouts  1.18 us (1%)
  other arithmetic  1.04 us (1%)
    pallas_call x1, Pallas kernels, on_device(): pl.pallas_call(functools.partial(attention_kernel, dims), out_shape=(jax....  89.6 us
    pallas_call x1, Pallas kernels, hand_over(): pl.pallas_call(kernel, out_shape=[jax.ShapeDtypeStruct(a.shape, a.dtype)...  3.03 us

profile of v6, /device:TPU:0, one launch (start us, length us, event | category | flops | bytes accessed | tf_op | source)
XLA Modules:
  0.0 95.5 jit_solution(3094333931044479323)
XLA Ops:
  0.6 0.0 copy-start
  0.7 0.0 copy-start.1
  0.7 0.7 copy-done.1
  1.4 0.2 dynamic-slice_reduce_fusion
  1.5 0.0 copy-done
  1.6 0.1 copy.13
  1.7 0.1 reshape.121
  1.8 0.1 iota_add_fusion
  1.8 0.1 add.103
  2.0 0.2 select_reduce_fusion
  2.1 0.1 select_reduce_fusion.1
  2.3 0.6 pad_add_fusion.table
  2.9 89.6 %shard_map.102 = (bf16[128,2048]{1,0:T(8,128)(2,1)}, bf16[128,2048]{1,0:T(8,128)(2,1)}, bf16[128,2048]{1,0:T(8,128)(2,1)}, f32[8,128]{1,0:T(8,128)}) custom-call(bf16[128,2048]{1,0:T(8,128)(2,1)} %bitcast.8, bf16[2,64,2048]{2,1,0:T(8,128)(2,1)} %bitcast.9, bf16[2,64,2048]{2,1,0:T(8,128)(2,1)} %bitcast.10, bf16[128,2048]{1,0:T(8,128)(2,1)} %bitcast.11, ...), custom_call_target="tpu_custom_call" | custom-call | flops 1342177280 | bytes 3670016 | tf_op jit(solution)/shard_map/pallas_call | solution.py:432
  92.5 3.0 %shard_map.103 = (bf16[128,2048]{1,0:T(8,128)(2,1)}, bf16[128,2048]{1,0:T(8,128)(2,1)}, bf16[128,2048]{1,0:T(8,128)(2,1)}, f32[1,16]{1,0:T(1,128)}) custom-call(bf16[128,2048]{1,0:T(8,128)(2,1)} %get-tuple-element.12.refs_0_, bf16[128,2048]{1,0:T(8,128)(2,1)} %get-tuple-element.13.refs_1_, bf16[128,2048]{1,0:T(8,128)(2,1)} %get-tuple-element.14.refs_2_, ...), custom_call_target="tpu_custom_call" | custom-call | tf_op jit(solution)/shard_map/pallas_call | solution.py:378
  (3 shorter events, 0.0 us)
Async XLA Ops:
  0.6 0.9 copy-start
  0.7 0.7 copy-start.1
